TPU v7x, 256 devices: a whole 4x4x8 slice. The times are simulated.
256 devices in a mesh: lat: 8 (over y_hi, x), lon: 32 (over z, y_lo, core).
Axes of the slice: x: 4, y: 4 (y_hi: 2, y_lo: 2; y = y_hi * 2 + y_lo), z: 8, core: 2. Of those that a mesh axis runs over, the one named last changes fastest.
Arguments:
- queries: bfloat16 [128, 256, 768], P('lat', 'lon'), may hold values from -8 to 8
- key_vectors: bfloat16 [128, 256, 768], P('lat', 'lon'), may hold values from -8 to 8
- value_vectors: bfloat16 [128, 256, 768], P('lat', 'lon'), may hold values from -12 to 12
- upstream: bfloat16 [128, 256, 768], P('lat', 'lon'), may hold values from -6 to 6
- w_out: bfloat16 [768, 768], replicated, may hold values from -0.21875 to 0.21875
- neighbours: int32 [16, 32, 4], replicated, may hold values from 0 to 511, as said below
- counts: int32 [16, 32], replicated, may hold values from 2 to 4, as said below
Outputs:
- mixed_out: bfloat16 [128, 256, 768], P('lat', 'lon')
- q_grad: bfloat16 [128, 256, 768], P('lat', 'lon')
- k_grad: bfloat16 [128, 256, 768], P('lat', 'lon')
- v_grad: bfloat16 [128, 256, 768], P('lat', 'lon')
- w_grad: float32 [768, 768], replicated
Inputs may be any that keep to these rules, and one draw needn't show every extreme that they name: `neighbours`: entry s of block (i, j) names a block i2 * 32 + j2 with i2 within one of i and j2 within one of j around the longitude circle; slot 0 names the block itself, the entries of slots below counts[i, j] are distinct, and the slots at or beyond counts[i, j] name the block itself. `counts`: every block outside the first and the last row of blocks has 4.
All inputs are finite; a program needn't handle non-finite values.
Results may differ from a plain program's by a relative error of at most 0.03.
Values may be sent and summed in bfloat16 or wider, within the bound.
A program may use at most 64 MiB of HBM per device.

v0:
```python
import math

import jax
import jax.numpy as jnp
from jax import lax
from jax.sharding import PartitionSpec as P

HEADS = 12
HEAD_DIM = 64
BLK = 8
SLOTS = 4


def padded_2(value, sides, width, wrap):
    for axis, dim in sides:
        peers, length = (lax.axis_size(axis), value.shape[dim])
        up = [(i, (i + 1) % peers) for i in range(peers if wrap else peers - 1)]
        down = [(j, i) for i, j in up]
        last = lax.slice_in_dim(value, length - width, length, axis=dim)
        leading = lax.slice_in_dim(value, 0, width, axis=dim)
        before = lax.ppermute(last, axis, up)
        after = lax.ppermute(leading, axis, down)
        value = jnp.concatenate([before, value, after], axis=dim)
    return value


def to_blocks(token_grid):
    lat_rows, lon_cols, feat_width = token_grid.shape
    block_tiles = token_grid.reshape(
        lat_rows // BLK, BLK, lon_cols // BLK, BLK, feat_width
    ).transpose(0, 2, 1, 3, 4)
    return block_tiles.reshape(lat_rows // BLK * (lon_cols // BLK), BLK * BLK, feat_width)


def from_blocks(block_tiles, lat_blocks, lon_blocks):
    feat_width = block_tiles.shape[-1]
    token_grid = block_tiles.reshape(lat_blocks, lon_blocks, BLK, BLK, feat_width).transpose(
        0, 2, 1, 3, 4
    )
    return token_grid.reshape(lat_blocks * BLK, lon_blocks * BLK, feat_width)


def split_heads(block_tiles):
    return block_tiles.reshape(block_tiles.shape[0], block_tiles.shape[1], HEADS, HEAD_DIM)


def slot_places(
    neighbours,
    counts,
    first_lat,
    first_lon,
    grid_rows,
    grid_cols,
    anchor_lat,
    anchor_lon,
    pad_rows,
    pad_cols,
):
    total_lat = neighbours.shape[0]
    total_lon = neighbours.shape[1]
    block_lat = first_lat + jnp.arange(grid_rows, dtype=jnp.int32)
    block_lon = (first_lon + jnp.arange(grid_cols, dtype=jnp.int32)) % total_lon
    inside = (block_lat >= 0) & (block_lat < total_lat)
    safe_lat = jnp.clip(block_lat, 0, total_lat - 1)
    slot_table = jnp.take(jnp.take(neighbours, safe_lat, axis=0), block_lon, axis=1)
    slot_limit = jnp.take(jnp.take(counts, safe_lat, axis=0), block_lon, axis=1)
    slot_ids = jnp.arange(SLOTS, dtype=jnp.int32)
    rel_lat = slot_table // total_lon - anchor_lat
    rel_lon = (slot_table % total_lon - anchor_lon) % total_lon
    usable = (slot_ids[None, None, :] < slot_limit[:, :, None]) & inside[:, None, None]
    usable = usable & (rel_lat >= 0) & (rel_lat < pad_rows) & (rel_lon < pad_cols)
    key_place = jnp.where(usable, rel_lat * pad_cols + rel_lon, 0)
    return (
        key_place.reshape(grid_rows * grid_cols, SLOTS),
        usable.reshape(grid_rows * grid_cols, SLOTS),
    )


def gather_sets(padded_tiles, key_place):
    picked = jnp.take(padded_tiles, key_place.reshape(-1), axis=0)
    return picked.reshape(key_place.shape[0], SLOTS * BLK * BLK, padded_tiles.shape[-1])


def masked_scores(query_tiles, key_sets, key_valid):
    raw = jnp.einsum(
        "nqhd,nkhd->nhqk",
        split_heads(query_tiles),
        split_heads(key_sets),
        preferred_element_type=jnp.float32,
    )
    raw = raw * (1.0 / math.sqrt(HEAD_DIM))
    return jnp.where(key_valid[:, None, None, :], raw, -jnp.inf)


def forward_core(query_tiles, key_sets, value_sets, key_valid):
    masked = masked_scores(query_tiles, key_sets, key_valid)
    row_top = jnp.max(masked, axis=-1, keepdims=True)
    exp_total = jnp.sum(jnp.exp(masked - row_top), axis=-1, keepdims=True)
    log_total = row_top + jnp.log(exp_total)
    attn_probs = jnp.exp(masked - log_total)
    probs_low = attn_probs.astype(jnp.bfloat16)
    mixed_heads = jnp.einsum(
        "nhqk,nkhd->nqhd", probs_low, split_heads(value_sets), preferred_element_type=jnp.float32
    )
    attended = mixed_heads.astype(jnp.bfloat16).reshape(query_tiles.shape)
    return (attended, attn_probs, probs_low, log_total[..., 0])


def head_delta(d_att, attended):
    product = d_att.astype(jnp.float32) * attended.astype(jnp.float32)
    return jnp.sum(split_heads(product), axis=-1).transpose(0, 2, 1)


def backward_scores(attn_probs, d_att, row_delta, value_sets):
    dprobs = jnp.einsum(
        "nqhd,nkhd->nhqk",
        split_heads(d_att),
        split_heads(value_sets),
        preferred_element_type=jnp.float32,
    )
    return (attn_probs * (dprobs - row_delta[..., None]) * (1.0 / math.sqrt(HEAD_DIM))).astype(
        jnp.bfloat16
    )


def grad_queries(dscores, key_sets):
    summed = jnp.einsum(
        "nhqk,nkhd->nqhd", dscores, split_heads(key_sets), preferred_element_type=jnp.float32
    )
    return summed.astype(jnp.bfloat16).reshape(summed.shape[0], summed.shape[1], -1)


def contract_keys(weights_low, block_tiles):
    summed = jnp.einsum(
        "nhqk,nqhd->nkhd", weights_low, split_heads(block_tiles), preferred_element_type=jnp.float32
    )
    return summed.reshape(summed.shape[0], summed.shape[1], -1)


def add_into(contrib, key_place, usable, pad_count):
    flat_place = key_place.reshape(-1)
    feat_width = contrib.shape[-1]
    flat_terms = contrib.reshape(flat_place.shape[0], BLK * BLK * feat_width)
    flat_terms = jnp.where(usable.reshape(-1)[:, None], flat_terms, 0.0)
    summed = (
        jnp.zeros((pad_count, BLK * BLK * feat_width), jnp.float32).at[flat_place].add(flat_terms)
    )
    return summed.reshape(pad_count, BLK * BLK, feat_width)


def fold_lat(extended, lat_rows):
    interior = extended[:, 2 * BLK : 2 * BLK + lat_rows]
    interior = interior.at[:, :BLK].add(extended[:, :BLK])
    return interior.at[:, lat_rows - BLK :].add(extended[:, lat_rows + 3 * BLK :])


def fold_lon(extended, lon_cols):
    interior = extended[:, :, 2 * BLK : 2 * BLK + lon_cols]
    interior = interior.at[:, :, :BLK].add(extended[:, :, :BLK])
    return interior.at[:, :, lon_cols - BLK :].add(extended[:, :, lon_cols + 3 * BLK :])


def on_device(queries, key_vectors, value_vectors, upstream, w_out, neighbours, counts):
    lat_rows, lon_cols, feat_width = queries.shape
    lat_blocks = lat_rows // BLK
    lon_blocks = lon_cols // BLK
    pad_rows = lat_blocks + 2
    pad_cols = lon_blocks + 2
    pad_count = pad_rows * pad_cols
    inner_count = BLK * BLK
    tokens_all = lat_rows * lon_cols * lax.axis_size("lat") * lax.axis_size("lon")
    first_lat = lax.axis_index("lat") * lat_blocks
    first_lon = lax.axis_index("lon") * lon_blocks
    stacked = jnp.stack((key_vectors, value_vectors))
    lon_wide = padded_2(stacked, (("lon", 2),), BLK, True)
    padded = padded_2(lon_wide, (("lat", 1),), BLK, False)
    key_tiles = to_blocks(padded[0])
    value_tiles = to_blocks(padded[1])
    own_place, own_usable = slot_places(
        neighbours,
        counts,
        first_lat,
        first_lon,
        lat_blocks,
        lon_blocks,
        first_lat - 1,
        first_lon - 1,
        pad_rows,
        pad_cols,
    )
    query_tiles = to_blocks(queries)
    key_sets = gather_sets(key_tiles, own_place)
    value_sets = gather_sets(value_tiles, own_place)
    key_valid = jnp.repeat(own_usable, inner_count, axis=1)
    attended, attn_probs, probs_low, log_total = forward_core(
        query_tiles, key_sets, value_sets, key_valid
    )
    flat_att = attended.reshape(-1, feat_width)
    mixed_flat = jnp.dot(flat_att, w_out, preferred_element_type=jnp.float32).astype(jnp.bfloat16)
    grad_tiles = to_blocks(upstream)
    flat_grad = grad_tiles.reshape(-1, feat_width)
    local_weight = lax.dot_general(
        flat_att, flat_grad, (((0,), (0,)), ((), ())), preferred_element_type=jnp.float32
    )
    w_grad = lax.psum(local_weight, ("lat", "lon")) / math.sqrt(tokens_all)
    d_att = lax.dot_general(
        flat_grad, w_out, (((1,), (1,)), ((), ())), preferred_element_type=jnp.float32
    )
    d_att = d_att.astype(jnp.bfloat16).reshape(attended.shape)
    row_delta = head_delta(d_att, attended)
    dscores = backward_scores(attn_probs, d_att, row_delta, value_sets)
    query_grad = grad_queries(dscores, key_sets)
    key_contrib = contract_keys(dscores, query_tiles)
    value_contrib = contract_keys(probs_low, d_att)
    key_pad = from_blocks(
        add_into(key_contrib, own_place, own_usable, pad_count), pad_rows, pad_cols
    )
    value_pad = from_blocks(
        add_into(value_contrib, own_place, own_usable, pad_count), pad_rows, pad_cols
    )
    pad_terms = jnp.stack((key_pad, value_pad))
    extended = padded_2(pad_terms.astype(jnp.bfloat16), (("lat", 1),), BLK, False).astype(
        pad_terms.dtype
    )
    rows_done = fold_lat(extended, lat_rows)
    extended_lon = padded_2(rows_done.astype(jnp.bfloat16), (("lon", 2),), BLK, True).astype(
        rows_done.dtype
    )
    folded = fold_lon(extended_lon, lon_cols)
    key_grad = folded[0].astype(jnp.bfloat16)
    value_grad = folded[1].astype(jnp.bfloat16)
    mixed_out = from_blocks(mixed_flat.reshape(attended.shape), lat_blocks, lon_blocks)
    q_grad = from_blocks(query_grad, lat_blocks, lon_blocks)
    return (mixed_out, q_grad, key_grad, value_grad, w_grad)


def solution(mesh):
    return jax.shard_map(
        on_device,
        mesh=mesh,
        in_specs=(
            P("lat", "lon", None),
            P("lat", "lon", None),
            P("lat", "lon", None),
            P("lat", "lon", None),
            P(),
            P(),
            P(),
        ),
        out_specs=(
            P("lat", "lon", None),
            P("lat", "lon", None),
            P("lat", "lon", None),
            P("lat", "lon", None),
            P(),
        ),
        check_vma=False,
    )
```

profile of v0, /device:TPU:1, one launch (start us, length us, event | category | flops | bytes accessed | tf_op | source)
XLA Modules:
  0.0 394.3 jit_solution(1990365408183735528)
XLA Ops:
  8.4 3.3 collective-permute-start.1
  15.1 1.5 convolution_convert_fusion.2
  16.6 4.0 %collective-permute-done = bf16[2,16,8,768]{3,2,1,0:T(8,128)(2,1)S(1)} collective-permute-done((bf16[2,16,8,768]{3,2,1,0:T(8,128)(2,1)S(1)}, bf16[2,16,8,768]{3,2,1,0:T(8,128)(2,1)S(1)}, u32[]{:S(2)}, u32[]{:S(2)}) %collective-permute-start) | collective-permute-done | bytes 393248 | tf_op jit(solution)/shard_map/ppermute | solution.py:21
  23.1 4.8 %collective-permute-start.2 = (bf16[2,8,24,768]{3,2,1,0:T(8,128)(2,1)}, bf16[2,8,24,768]{3,2,1,0:T(8,128)(2,1)}, u32[]{:S(2)}, u32[]{:S(2)}) collective-permute-start(bf16[2,8,24,768]{3,2,1,0:T(8,128)(2,1)} %get-tuple-element.101), channel_id=1, source_target_pairs={{0,32},{32,64},{64,96},{96,128},{128,160},{160,192},{192,224},{1,3... | collective-permute-start | bytes 1769480 | tf_op jit(solution)/shard_map/ppermute | solution.py:21
  31.9 2.0 collective-permute-done.3
  36.6 1.5 gather_fusion.3
  38.1 1.5 gather_fusion.2
  39.6 2.5 broadcast_select_fusion.2
  42.1 2.7 reshape.642
  44.8 2.1 copy.37
  47.0 2.7 reshape.643
  49.7 2.1 copy.35
  51.9 1.8 bitcast_reduce_fusion
  58.2 1.5 convolution_bitcast_fusion
  59.7 4.7 %copy.46 = f32[2,256,12,64]{3,2,1,0:T(8,128)} copy(f32[2,256,12,64]{1,3,2,0:T(8,128)} %convolution_bitcast_fusion) | data formatting | bytes 3145728 | tf_op jit(solution)/shard_map/nhqk,nqhd->nkhd/transpose | solution.py:134
  64.4 4.4 %reshape_reshape.37 = f32[8,49152]{1,0:T(8,128)} reshape(f32[2,256,12,64]{3,2,1,0:T(8,128)} %copy.46) | data formatting | bytes 3145728 | tf_op jit(solution)/shard_map/reshape;reshape | solution.py:143
  68.8 3.7 copy.49
  72.5 4.5 %reshape_reshape.39 = f32[8,49152]{1,0:T(8,128)} reshape(f32[2,256,12,64]{3,2,1,0:T(8,128)} %copy.49) | data formatting | bytes 3145728 | tf_op jit(solution)/shard_map/reshape;reshape | solution.py:143
  77.1 3.4 broadcast_select_fusion.1
  80.5 5.1 %scatter_custom_fusion.1 = f32[12,49152]{1,0:T(8,128)} fusion(s32[8]{0:T(128)} %fusion.29, f32[8,49152]{1,0:T(8,128)} %get-tuple-element.106, f32[]{:T(128)} %constant.271.clone.1), kind=kCustom, calls=%fused_computation.14 | custom fusion | flops 393216 | bytes 2359808 | tf_op jit(solution)/shard_map/scatter-add | solution.py:146
  85.6 2.0 convert.17
  88.1 4.9 %scatter_custom_fusion = f32[12,49152]{1,0:T(8,128)} fusion(s32[8]{0:T(128)} %fusion.29, f32[8,49152]{1,0:T(8,128)} %get-tuple-element.105, f32[]{:T(128)} %constant.271.clone.1), kind=kCustom, calls=%fused_computation.16 | custom fusion | flops 393216 | bytes 2359808 | tf_op jit(solution)/shard_map/scatter-add | solution.py:146
  93.0 2.0 convert.16
  98.0 5.5 %collective-permute-start.4 = (bf16[2,8,24,768]{3,2,1,0:T(8,128)(2,1)}, bf16[2,8,24,768]{3,2,1,0:T(8,128)(2,1)}, u32[]{:S(2)}, u32[]{:S(2)}) collective-permute-start(bf16[2,8,24,768]{3,2,1,0:T(8,128)(2,1)} %get-tuple-element.95), channel_id=1, source_target_pairs={{0,32},{32,64},{64,96},{96,128},{128,160},{160,192},{192,224},{1,3... | collective-permute-start | bytes 1769480 | tf_op jit(solution)/shard_map/ppermute | solution.py:21
  104.7 1.9 reshape_reshape.35
  106.7 2.9 fusion.17
  109.9 1.7 maximum_convert_fusion
  115.4 7.0 %collective-permute-start.7 = (bf16[2,16,8,768]{3,2,1,0:T(8,128)(2,1)}, bf16[2,16,8,768]{3,2,1,0:T(8,128)(2,1)}, u32[]{:S(2)}, u32[]{:S(2)}) collective-permute-start(bf16[2,16,8,768]{3,2,1,0:T(8,128)(2,1)} %get-tuple-element.100), channel_id=1, source_target_pairs={{1,0},{2,1},{3,2},{4,3},{5,4},{6,5},{7,6},{8,7},{9,8},{10,9},{11,1... | collective-permute-start | bytes 1179656 | tf_op jit(solution)/shard_map/ppermute | solution.py:22
  125.3 4.2 %collective-permute-done.7 = bf16[2,16,8,768]{3,2,1,0:T(8,128)(2,1)} collective-permute-done((bf16[2,16,8,768]{3,2,1,0:T(8,128)(2,1)}, bf16[2,16,8,768]{3,2,1,0:T(8,128)(2,1)}, u32[]{:S(2)}, u32[]{:S(2)}) %collective-permute-start.7) | collective-permute-done | bytes 393248 | tf_op jit(solution)/shard_map/ppermute | solution.py:22
  129.4 4.8 %collective-permute-done.6 = bf16[2,16,8,768]{3,2,1,0:T(8,128)(2,1)} collective-permute-done((bf16[2,16,8,768]{3,2,1,0:T(8,128)(2,1)}, bf16[2,16,8,768]{3,2,1,0:T(8,128)(2,1)}, u32[]{:S(2)}, u32[]{:S(2)}) %collective-permute-start.6) | collective-permute-done | bytes 393248 | tf_op jit(solution)/shard_map/ppermute | solution.py:21
  136.3 247.8 %all-reduce.2.cloned.1.call-done = f32[768,768]{1,0:T(8,128)} async-done(((f32[768,768]{1,0:T(8,128)}), f32[768,768]{1,0:T(8,128)}) %all-reduce.2.cloned.1.call-update) | async-done | bytes 2359312 | tf_op jit(solution)/shard_map/psum | solution.py:205
  384.1 3.3 broadcast_multiply_fusion
  (93 shorter events, 31.6 us)
Async XLA Ops:
  7.2 7.9 %copy-start = (bf16[768,768]{1,0:T(8,128)(2,1)S(1)}, bf16[768,768]{1,0:T(8,128)(2,1)}, u32[]{:S(2)}) copy-start(bf16[768,768]{1,0:T(8,128)(2,1)} %param.25) | copy-start | bytes 3538948
  7.2 13.5 %copy-start.9 = (bf16[16,8,768]{2,1,0:T(8,128)(2,1)S(1)}, bf16[16,8,768]{2,1,0:T(8,128)(2,1)}, u32[]{:S(2)}) copy-start(bf16[16,8,768]{2,1,0:T(8,128)(2,1)} %param.23) | copy-start | bytes 589828
  7.2 13.5 %copy-start.10 = (bf16[16,8,768]{2,1,0:T(8,128)(2,1)S(1)}, bf16[16,8,768]{2,1,0:T(8,128)(2,1)}, u32[]{:S(2)}) copy-start(bf16[16,8,768]{2,1,0:T(8,128)(2,1)} %param.22) | copy-start | bytes 589828
  7.2 376.9 %all-reduce.2.cloned.1.call-start = ((), (), s32[]{:S(2)}) async-start(), calls=%async_computation | async-start | bytes 4718592 | tf_op jit(solution)/shard_map/psum | solution.py:205
  8.4 8.2 %collective-permute-start.1 = (bf16[2,16,8,768]{3,2,1,0:T(8,128)(2,1)S(1)}, bf16[2,16,8,768]{3,2,1,0:T(8,128)(2,1)S(1)}, u32[]{:S(2)}, u32[]{:S(2)}) collective-permute-start(bf16[2,16,8,768]{3,2,1,0:T(8,128)(2,1)S(1)} %pad_maximum_fusion.6), channel_id=1, source_target_pairs={{1,0},{2,1},{3,2},{4,3},{5,4},{6,5},{7,6},{8,7},{9,8},{10,9},{11,1... | collective-permute-start | bytes 1179656 | tf_op jit(solution)/shard_map/ppermute | solution.py:22
  11.7 8.9 %collective-permute-start = (bf16[2,16,8,768]{3,2,1,0:T(8,128)(2,1)S(1)}, bf16[2,16,8,768]{3,2,1,0:T(8,128)(2,1)S(1)}, u32[]{:S(2)}, u32[]{:S(2)}) collective-permute-start(bf16[2,16,8,768]{3,2,1,0:T(8,128)(2,1)S(1)} %pad_maximum_fusion.6), channel_id=1, source_target_pairs={{0,1},{1,2},{2,3},{3,4},{4,5},{5,6},{6,7},{7,8},{8,9},{9,10},{10,1... | collective-permute-start | bytes 1179656 | tf_op jit(solution)/shard_map/ppermute | solution.py:21
  20.8 8.9 %copy-start.13 = (bf16[16,8,768]{2,1,0:T(8,128)(2,1)S(1)}, bf16[16,8,768]{2,1,0:T(8,128)(2,1)}, u32[]{:S(2)}) copy-start(bf16[16,8,768]{2,1,0:T(8,128)(2,1)} %param.21) | copy-start | bytes 589828
  21.9 12.1 %collective-permute-start.3 = (bf16[2,8,24,768]{3,2,1,0:T(8,128)(2,1)}, bf16[2,8,24,768]{3,2,1,0:T(8,128)(2,1)}, u32[]{:S(2)}, u32[]{:S(2)}) collective-permute-start(bf16[2,8,24,768]{3,2,1,0:T(8,128)(2,1)} %get-tuple-element.102), channel_id=1, source_target_pairs={{32,0},{64,32},{96,64},{128,96},{160,128},{192,160},{224,192},{33,... | collective-permute-start | bytes 1769480 | tf_op jit(solution)/shard_map/ppermute | solution.py:22
  23.1 11.7 %collective-permute-start.2 = (bf16[2,8,24,768]{3,2,1,0:T(8,128)(2,1)}, bf16[2,8,24,768]{3,2,1,0:T(8,128)(2,1)}, u32[]{:S(2)}, u32[]{:S(2)}) collective-permute-start(bf16[2,8,24,768]{3,2,1,0:T(8,128)(2,1)} %get-tuple-element.101), channel_id=1, source_target_pairs={{0,32},{32,64},{64,96},{96,128},{128,160},{160,192},{192,224},{1,3... | collective-permute-start | bytes 1769480 | tf_op jit(solution)/shard_map/ppermute | solution.py:21
  38.1 1.5 copy-start.8
  51.9 2.4 copy-start.5
  54.2 1.1 copy-start.3
  56.6 1.6 copy-start.7
  57.3 0.9 copy-start.1
  72.5 4.6 %copy-start.6 = (f32[8,49152]{1,0:T(8,128)S(1)}, f32[8,49152]{1,0:T(8,128)}, u32[]{:S(2)}) copy-start(f32[8,49152]{1,0:T(8,128)} %reshape_reshape.37) | copy-start | bytes 4718596
  95.6 8.0 %copy-start.12 = (bf16[2,64,12,64]{1,3,2,0:T(8,128)(2,1)S(1)}, bf16[2,64,12,64]{1,3,2,0:T(8,128)(2,1)}, u32[]{:S(2)}) copy-start(bf16[2,64,12,64]{1,3,2,0:T(8,128)(2,1)} %get-tuple-element.114) | copy-start | bytes 589828
  96.8 12.8 %collective-permute-start.5 = (bf16[2,8,24,768]{3,2,1,0:T(8,128)(2,1)}, bf16[2,8,24,768]{3,2,1,0:T(8,128)(2,1)}, u32[]{:S(2)}, u32[]{:S(2)}) collective-permute-start(bf16[2,8,24,768]{3,2,1,0:T(8,128)(2,1)} %get-tuple-element.96), channel_id=1, source_target_pairs={{32,0},{64,32},{96,64},{128,96},{160,128},{192,160},{224,192},{33,... | collective-permute-start | bytes 1769480 | tf_op jit(solution)/shard_map/ppermute | solution.py:22
  98.0 11.9 %collective-permute-start.4 = (bf16[2,8,24,768]{3,2,1,0:T(8,128)(2,1)}, bf16[2,8,24,768]{3,2,1,0:T(8,128)(2,1)}, u32[]{:S(2)}, u32[]{:S(2)}) collective-permute-start(bf16[2,8,24,768]{3,2,1,0:T(8,128)(2,1)} %get-tuple-element.95), channel_id=1, source_target_pairs={{0,32},{32,64},{64,96},{96,128},{128,160},{160,192},{192,224},{1,3... | collective-permute-start | bytes 1769480 | tf_op jit(solution)/shard_map/ppermute | solution.py:21
  114.5 8.0 %copy-start.2 = (bf16[2,12,64,256]{3,2,1,0:T(8,128)(2,1)S(1)}, bf16[2,12,64,256]{3,2,1,0:T(8,128)(2,1)}, u32[]{:S(2)}) copy-start(bf16[2,12,64,256]{3,2,1,0:T(8,128)(2,1)} %copy-done.1) | copy-start | bytes 2359300
  114.5 8.0 %copy-start.4 = (bf16[2,256,12,64]{1,3,2,0:T(8,128)(2,1)S(1)}, bf16[2,256,12,64]{1,3,2,0:T(8,128)(2,1)}, u32[]{:S(2)}) copy-start(bf16[2,256,12,64]{1,3,2,0:T(8,128)(2,1)} %copy.35) | copy-start | bytes 2359300
  115.4 14.0 %collective-permute-start.7 = (bf16[2,16,8,768]{3,2,1,0:T(8,128)(2,1)}, bf16[2,16,8,768]{3,2,1,0:T(8,128)(2,1)}, u32[]{:S(2)}, u32[]{:S(2)}) collective-permute-start(bf16[2,16,8,768]{3,2,1,0:T(8,128)(2,1)} %get-tuple-element.100), channel_id=1, source_target_pairs={{1,0},{2,1},{3,2},{4,3},{5,4},{6,5},{7,6},{8,7},{9,8},{10,9},{11,1... | collective-permute-start | bytes 1179656 | tf_op jit(solution)/shard_map/ppermute | solution.py:22
  122.4 1.8 copy-start.11
  122.4 11.8 %collective-permute-start.6 = (bf16[2,16,8,768]{3,2,1,0:T(8,128)(2,1)}, bf16[2,16,8,768]{3,2,1,0:T(8,128)(2,1)}, u32[]{:S(2)}, u32[]{:S(2)}) collective-permute-start(bf16[2,16,8,768]{3,2,1,0:T(8,128)(2,1)} %get-tuple-element.99), channel_id=1, source_target_pairs={{0,1},{1,2},{2,3},{3,4},{4,5},{5,6},{6,7},{7,8},{8,9},{9,10},{10,1... | collective-permute-start | bytes 1179656 | tf_op jit(solution)/shard_map/ppermute | solution.py:21
Sparse Core Ops, SparseCore 0:
  109.7 274.4 all-reduce.1
where the time goes:
time: 396 us; the launch traced here: 394 us
  waiting for transfers between devices  264 us (67%)
  local copies, waits for them, and re-layouts  46.5 us (12%)
  other arithmetic  34.4 us (9%)
  starting transfers between devices  23.3 us (6%)
  between operations  14.4 us (4%)
  matrix products  11.4 us (3%)
    psum x1, waiting for transfers between devices, on_device(): w_grad = lax.psum(local_weight, ('lat', 'lon')) / math.sqrt(tokens_all)  248 us
    ppermute x4, starting transfers between devices, padded_2(): after = lax.ppermute(leading, axis, down)  12.9 us
    another operation x8, local copies, waits for them, and re-layouts, split_heads(): block_tiles.reshape(block_tiles.shape[0], block_tiles.shape[1], HEADS, HE...  12.7 us
    ppermute x4, starting transfers between devices, padded_2(): before = lax.ppermute(last, axis, up)  10.4 us
    ppermute x4, waiting for transfers between devices, padded_2(): before = lax.ppermute(last, axis, up)  10.1 us
    scatter-add x2, other arithmetic, add_into(): jnp.zeros((pad_count, BLK * BLK * feat_width), jnp.float32).at[flat_place]  10 us
    another operation x2, local copies, waits for them, and re-layouts, add_into(): flat_terms = contrib.reshape(flat_place.shape[0], BLK * BLK * feat_width)  8.94 us
    transpose x2, local copies, waits for them, and re-layouts, contract_keys(): jnp.einsum('nhqk,nqhd->nkhd', weights_low, split_heads(block_tiles), pref...  8.45 us
  transfers between devices with their start and end apart: 9, of which 8 were waited for; matrix products, arithmetic and copies ran while one was open for 6% of the time, Pallas kernels for 0%

commit v1 on v0

v1 whole, which is shorter than its diff:
```python
import math

import jax
import jax.numpy as jnp
from jax import lax
from jax.experimental import pallas as pl
from jax.experimental.pallas import tpu as pltpu
from jax.sharding import PartitionSpec as P

F32 = jnp.float32
BF16 = jnp.bfloat16
MESH = pl.DeviceIdType.MESH

HEAD_DIM = 64
SLOTS = 4
TOK = 64
D = 768
PAIRS = 6
NLON = 32
NLAT = 8
TOKENS = 32768
HALF = D // 2
GROUP = 16
FLAT = HALF * (D // 128)
CHUNK = FLAT // GROUP
OWNERS = 3
PIECE = CHUNK // OWNERS
DEPTH = 8
NT = (((1,), (1,)), ((), ()))
TN = (((0,), (0,)), ((), ()))


def remote(src, dst, send_sem, recv_sem, device):
    return pltpu.make_async_remote_copy(
        src_ref=src,
        dst_ref=dst,
        send_sem=send_sem,
        recv_sem=recv_sem,
        device_id=device,
        device_id_type=MESH,
    )


def kernel(
    q_ref,
    k_ref,
    v_ref,
    u_ref,
    w_ref,
    nb_ref,
    ct_ref,
    mixed_ref,
    dq_ref,
    dk_ref,
    dv_ref,
    wg_ref,
    kvb,
    ucat,
    datt,
    probs,
    att2,
    att_in,
    att_t,
    cb,
    gsp,
    grp,
    gsl,
    grl,
    gso,
    gro,
    wbuf,
    rsin,
    zsum,
    zin,
    wch,
    wfin,
    halo_s,
    halo_r,
    u_s,
    u_r,
    gp_s,
    gp_r,
    gl_s,
    gl_r,
    go_s,
    go_r,
    rs_s,
    rs_r,
    z_s,
    z_r,
    zg_s,
    zg_r,
    ag_s,
    ag_r,
    fw_s,
    fw_r,
):
    a = lax.axis_index("lat")
    b = lax.axis_index("lon")
    core = lax.rem(b, 2)
    ylo = lax.rem(b // 2, 2)
    z = b // 4
    has_up = a > 0
    has_down = a < NLAT - 1
    mate = (a, b + 1 - 2 * core)
    beyond = (a, lax.rem(b + NLON - 1 + 2 * core, NLON))
    up = (a - 1, b)
    down = (a + 1, b)
    oc = 2 * core
    ic = 2 - oc
    n = a * 2 + ylo

    def peer(k):
        m = lax.rem(n + k, GROUP)
        return (m // 2, z * 4 + lax.rem(m, 2) * 2 + core), m

    def zpeer(zz):
        return (a, zz * 4 + ylo * 2 + core)

    barrier = pltpu.get_barrier_semaphore()

    def greet(device):
        pl.semaphore_signal(barrier, inc=1, device_id=device, device_id_type=MESH)

    greet(mate)
    greet(beyond)

    @pl.loop(1, GROUP)
    def _(k):
        greet(peer(k)[0])

    @pl.loop(1, DEPTH)
    def _(k):
        greet(zpeer(lax.rem(z + k, DEPTH)))

    kvb[0, 1, 1:3] = k_ref[...]
    kvb[1, 1, 1:3] = v_ref[...]
    ucat[0:128] = u_ref[...]
    pl.semaphore_wait(barrier, 2 + GROUP - 1 + DEPTH - 1)

    def halo(t, i, src, dst, device):
        return remote(src, dst, halo_s.at[t, i], halo_r.at[t, i], device)

    ins = (k_ref, v_ref)

    def first(t):
        src = ins[t]
        return (
            halo(t, 1, src, kvb.at[t, ic, pl.ds(1, 2)], beyond),
            halo(t, 2, src.at[0], kvb.at[t, 1, 3], up),
            halo(t, 3, src.at[1], kvb.at[t, 1, 0], down),
            halo(t, 0, src, kvb.at[t, oc, pl.ds(1, 2)], mate),
        )

    def second(t):
        return (
            halo(t, 4, kvb.at[t, oc, 1], kvb.at[t, oc, 3], up),
            halo(t, 5, kvb.at[t, oc, 2], kvb.at[t, oc, 0], down),
            halo(t, 6, kvb.at[t, 1, 0], kvb.at[t, oc, 0], mate),
            halo(t, 7, kvb.at[t, 1, 3], kvb.at[t, oc, 3], mate),
        )

    for t in range(2):
        c = first(t)
        c[0].start()
        pl.when(has_up)(c[1].start)
        pl.when(has_down)(c[2].start)
        c[3].start()
    send_u = remote(u_ref, ucat.at[pl.ds(128, 128)], u_s.at[0], u_r.at[0], mate)
    send_u.start()

    datt[...] = lax.dot_general(
        u_ref[...], w_ref[...], NT, preferred_element_type=F32
    ).astype(BF16)
    for t in range(2):
        for s in range(2):
            cb[t, s, SLOTS] = jnp.zeros((TOK, D), F32)

    for t in range(2):
        c = second(t)
        halo(t, 1, k_ref, kvb.at[t, oc, pl.ds(1, 2)], beyond).wait_recv()
        pl.when(has_up)(c[0].start)
        pl.when(has_down)(c[1].start)

        @pl.when(has_up)
        def _():
            halo(t, 3, k_ref.at[0], kvb.at[t, 1, 0], up).wait_recv()
            c[2].start()

        @pl.when(has_down)
        def _():
            halo(t, 2, k_ref.at[0], kvb.at[t, 1, 3], down).wait_recv()
            c[3].start()

    for t in range(2):
        halo(t, 0, k_ref, kvb.at[t, ic, pl.ds(1, 2)], mate).wait_recv()

        @pl.when(has_up)
        def _():
            halo(t, 5, k_ref.at[0], kvb.at[t, oc, 0], up).wait_recv()
            halo(t, 6, k_ref.at[0], kvb.at[t, ic, 0], mate).wait_recv()

        @pl.when(has_down)
        def _():
            halo(t, 4, k_ref.at[0], kvb.at[t, oc, 3], down).wait_recv()
            halo(t, 7, k_ref.at[0], kvb.at[t, ic, 3], mate).wait_recv()

    def places(s_block):
        i = 2 * a + s_block
        out = []
        for s in range(SLOTS):
            name = nb_ref[i, b, s]
            row = lax.div(name, NLON) - i + 1
            col = lax.rem(lax.rem(name, NLON) - b + 1 + NLON, NLON)
            out.append((jnp.clip(col, 0, 2), jnp.clip(row, 0, 2)))
        return out, ct_ref[i, b]

    def blocks_of(t, place, s_block, j):
        return jnp.concatenate(
            [kvb[t, col, row + s_block, :, pl.ds(j * 128, 128)] for col, row in place], axis=0
        )

    low = lax.broadcasted_iota(jnp.int32, (TOK, 128), 1) < HEAD_DIM

    def stacked(x):
        zero = jnp.zeros_like(x)
        return jnp.concatenate([jnp.where(low, x, zero), jnp.where(low, zero, x)], axis=0)

    def queries_of(s_block, j):
        x = q_ref[s_block, :, pl.ds(j * 128, 128)]
        return stacked(x * jnp.asarray(0.125, BF16))

    def unstacked(x):
        return jnp.where(low, x[:TOK], x[TOK:])

    @pl.loop(0, 2)
    def _(s):
        place, count = places(s)
        kept = lax.broadcasted_iota(jnp.int32, (2 * TOK, SLOTS * TOK), 1) < count * TOK
        rows = pl.ds(pl.multiple_of(s * TOK, TOK), TOK)
        scores = []
        for j in range(PAIRS):
            scores.append(
                lax.dot_general(
                    queries_of(s, j), blocks_of(0, place, s, j), NT, preferred_element_type=F32
                )
            )
        for j in range(PAIRS):
            masked = jnp.where(kept, scores[j], -1e30)
            top = jnp.max(masked, axis=-1, keepdims=True)
            e = jnp.exp(masked - top)
            probs[s, j] = e * (1.0 / jnp.sum(e, axis=-1, keepdims=True))
        for j in range(PAIRS):
            o = jnp.dot(
                probs[s, j].astype(BF16), blocks_of(1, place, s, j), preferred_element_type=F32
            )
            att2[j // 3, rows, (j % 3) * 128 : (j % 3) * 128 + 128] = unstacked(o).astype(BF16)

    send_att = remote(att2.at[1 - core], att_in, u_s.at[1], u_r.at[1], mate)
    send_att.start()
    att_t[:, 0:128] = att2[core].T
    att = jnp.concatenate([att2[0], att2[1]], axis=1)
    mixed_ref[...] = jnp.dot(att, w_ref[...], preferred_element_type=F32).astype(BF16)
    remote(u_ref, ucat.at[pl.ds(128, 128)], u_s.at[0], u_r.at[0], mate).wait_recv()
    send_att.wait_recv()
    att_t[:, 128:256] = att_in[...].T
    for g in range(3):
        term = jnp.dot(
            att_t[...], ucat[:, g * 256 : g * 256 + 256], preferred_element_type=F32
        ).astype(BF16)
        wbuf[2 * g * HALF : (2 * g + 1) * HALF] = term[:, :128]
        wbuf[(2 * g + 1) * HALF : (2 * g + 2) * HALF] = term[:, 128:]

    def chunk(m):
        return pl.ds(pl.multiple_of(m * CHUNK, 16), CHUNK)

    def reduce_copy(k):
        device, m = peer(k)
        return remote(wbuf.at[chunk(m)], rsin.at[k], rs_s.at[k], rs_r.at[k], device)

    @pl.loop(1, GROUP)
    def _(k):
        reduce_copy(k).start()

    @pl.loop(0, 2)
    def _(s):
        place, _ = places(s)
        rows = pl.ds(pl.multiple_of(s * TOK, TOK), TOK)
        for j in range(PAIRS):
            lanes = pl.ds(j * 128, 128)
            qs = queries_of(s, j)
            ks = blocks_of(0, place, s, j)
            vs = blocks_of(1, place, s, j)
            da = stacked(datt[rows, lanes])
            at = att2[j // 3, rows, (j % 3) * 128 : (j % 3) * 128 + 128]
            at = jnp.concatenate([at, at], axis=0)
            delta = jnp.sum(da.astype(F32) * at.astype(F32), axis=-1, keepdims=True)
            p = probs[s, j]
            dp = lax.dot_general(da, vs, NT, preferred_element_type=F32)
            ds = (p * (dp - delta)).astype(BF16)
            dq = unstacked(jnp.dot(ds, ks, preferred_element_type=F32)) * 0.125
            dq_ref[s, :, lanes] = dq.astype(BF16)
            dk = lax.dot_general(ds, qs, TN, preferred_element_type=F32)
            dv = lax.dot_general(p.astype(BF16), da, TN, preferred_element_type=F32)
            for i in range(SLOTS):
                cb[0, s, i, :, lanes] = dk[i * TOK : (i + 1) * TOK]
                cb[1, s, i, :, lanes] = dv[i * TOK : (i + 1) * TOK]

    placed = [places(s) for s in range(2)]

    def slot_of(s, row, col):
        slot = jnp.int32(SLOTS)
        place, count = placed[s]
        for i in range(SLOTS):
            hit = (place[i][0] == col) & (place[i][1] == row) & (i < count)
            slot = jnp.where(hit, i, slot)
        return slot

    def terms(t, col, row):
        total = None
        for s in range(2):
            if 0 <= row - s <= 2:
                x = cb[t, s, slot_of(s, row - s, col)]
                total = x if total is None else total + x
        return total

    def to_mate(t):
        return remote(gsp.at[t], grp.at[t], gp_s.at[t], gp_r.at[t], mate)

    def to_lat(t, way, which):
        device = (up, down)[way]
        return remote(
            gsl.at[t, way, which],
            grl.at[t, way, which],
            gl_s.at[t, way, which],
            gl_r.at[t, way, which],
            device,
        )

    def to_beyond(t):
        return remote(gso.at[t], gro.at[t], go_s.at[t], go_r.at[t], beyond)

    conds = (has_up, has_down)
    from_conds = (has_down, has_up)
    for t in range(2):
        for r in range(4):
            gsp[t, r] = terms(t, ic, r).astype(BF16)
        to_mate(t).start()
        for way in range(2):

            @pl.when(conds[way])
            def _():
                gsl[t, way, 0] = terms(t, oc, 3 * way).astype(BF16)
                to_lat(t, way, 0).start()

    total = wbuf[chunk(n), :].astype(F32)
    for k in range(1, GROUP):
        reduce_copy(k).wait_recv()
        total = total + rsin[k].astype(F32)
    zsum[...] = total.astype(BF16)

    def owner_z(o):
        return 3 * o

    def z_copy(o):
        k = lax.rem(owner_z(o) - z + DEPTH, DEPTH)
        return remote(
            zsum.at[pl.ds(o * PIECE, PIECE)], zin.at[k], z_s.at[o], z_r.at[k], zpeer(owner_z(o))
        )

    for o in range(OWNERS):
        pl.when(z != owner_z(o))(z_copy(o).start)

    for t in range(2):
        to_mate(t).wait_recv()
        for way in range(2):

            @pl.when(conds[way])
            def _():
                x = terms(t, 1, 3 * way) + grp[t, 3 * way].astype(F32)
                gsl[t, way, 1] = x.astype(BF16)
                to_lat(t, way, 1).start()

    def z_gather(o, k):
        return remote(
            wch.at[pl.ds(o * PIECE, PIECE)],
            wch.at[pl.ds(o * PIECE, PIECE)],
            zg_s.at[k],
            zg_r.at[o],
            zpeer(lax.rem(owner_z(o) + k, DEPTH)),
        )

    for o in range(OWNERS):

        @pl.when(z == owner_z(o))
        def _():
            acc = zsum[o * PIECE : (o + 1) * PIECE].astype(F32)
            for k in range(1, DEPTH):
                remote(
                    zsum.at[pl.ds(o * PIECE, PIECE)],
                    zin.at[k],
                    z_s.at[o],
                    z_r.at[k],
                    zpeer(lax.rem(z + DEPTH - k, DEPTH)),
                ).wait_recv()
                acc = acc + zin[k].astype(F32)
            wch[o * PIECE : (o + 1) * PIECE] = (acc * (1.0 / math.sqrt(TOKENS))).astype(BF16)
            for k in range(1, DEPTH):
                z_gather(o, k).start()

    for t in range(2):
        for r in range(2):
            x = terms(t, oc, 1 + r)
            gso[t, r] = x.astype(BF16)
        for way in range(2):

            @pl.when(from_conds[way])
            def _():
                to_lat(t, way, 0).wait_recv()
                r = 1 - way
                x = terms(t, oc, 1 + r) + grl[t, way, 0].astype(F32)
                gso[t, r] = x.astype(BF16)

        to_beyond(t).start()

    for o in range(OWNERS):
        pl.when(z != owner_z(o))(z_gather(o, 1).wait_recv)

    def gather_copy(k):
        device, _ = peer(k)
        return remote(wch, wfin.at[core, chunk(n)], ag_s.at[k], ag_r.at[k], device)

    @pl.loop(1, GROUP)
    def _(k):
        gather_copy(k).start()

    wfin[core, chunk(n), :] = wch[...]

    def pass_on(k, half):
        m = lax.rem(n + GROUP - k, GROUP)
        return remote(
            wfin.at[half, chunk(m)], wfin.at[half, chunk(m)], fw_s.at[k], fw_r.at[k], mate
        )

    pass_on(0, core).start()

    outs = (dk_ref, dv_ref)
    for t in range(2):
        to_beyond(t).wait_recv()
        for r in range(2):
            x = terms(t, 1, 1 + r) + grp[t, 1 + r].astype(F32) + gro[t, r].astype(F32)
            outs[t][r] = x.astype(BF16)
        for way in range(2):

            @pl.when(from_conds[way])
            def _():
                to_lat(t, way, 1).wait_recv()
                r = 1 - way
                x = terms(t, 1, 1 + r) + grp[t, 1 + r].astype(F32) + gro[t, r].astype(F32)
                outs[t][r] = (x + grl[t, way, 1].astype(F32)).astype(BF16)

    @pl.loop(1, GROUP)
    def _(k):
        m = lax.rem(n + GROUP - k, GROUP)
        device = (m // 2, z * 4 + lax.rem(m, 2) * 2 + core)
        remote(wch, wfin.at[core, chunk(m)], ag_s.at[k], ag_r.at[k], device).wait_recv()
        pass_on(k, core).start()

    rows_of = pl.ds(pl.multiple_of(core * HALF, HALF), HALF)
    for g in range(D // 128):
        wg_ref[rows_of, g * 128 : g * 128 + 128] = wfin[
            core, g * HALF : (g + 1) * HALF
        ].astype(F32)

    @pl.loop(0, GROUP)
    def _(k):
        pass_on(k, 1 - core).wait_recv()

    rows_of = pl.ds(pl.multiple_of((1 - core) * HALF, HALF), HALF)
    for g in range(D // 128):
        wg_ref[rows_of, g * 128 : g * 128 + 128] = wfin[
            1 - core, g * HALF : (g + 1) * HALF
        ].astype(F32)

    for t in range(2):
        c = first(t)
        c[0].wait_send()
        c[3].wait_send()
        d = second(t)
        for x in (c[1], d[0], d[2]):
            pl.when(has_up)(x.wait_send)
        for x in (c[2], d[1], d[3]):
            pl.when(has_down)(x.wait_send)
        to_mate(t).wait_send()
        to_beyond(t).wait_send()
        for way in range(2):
            for which in range(2):
                pl.when(conds[way])(to_lat(t, way, which).wait_send)
    send_u.wait_send()
    send_att.wait_send()
    for o in range(OWNERS):
        pl.when(z != owner_z(o))(z_copy(o).wait_send)

        @pl.when(z == owner_z(o))
        def _():
            for k in range(1, DEPTH):
                z_gather(o, k).wait_send()

    @pl.loop(1, GROUP)
    def _(k):
        reduce_copy(k).wait_send()
        gather_copy(k).wait_send()

    @pl.loop(0, GROUP)
    def _(k):
        pass_on(k, core).wait_send()


def on_device(queries, key_vectors, value_vectors, upstream, w_out, neighbours, counts):
    shape = queries.shape
    vmem = pl.BlockSpec(memory_space=pltpu.VMEM)
    smem = pl.BlockSpec(memory_space=pltpu.SMEM)
    blocks = jax.ShapeDtypeStruct((2, TOK, D), BF16)
    dma = pltpu.SemaphoreType.DMA
    mixed, dq, dk, dv, wg = pl.pallas_call(
        kernel,
        out_shape=(
            jax.ShapeDtypeStruct((2 * TOK, D), BF16),
            blocks,
            blocks,
            blocks,
            jax.ShapeDtypeStruct((D, D), F32),
        ),
        in_specs=[vmem] * 5 + [smem] * 2,
        out_specs=(vmem,) * 5,
        scratch_shapes=[
            pltpu.VMEM((2, 3, 4, TOK, D), BF16),
            pltpu.VMEM((256, D), BF16),
            pltpu.VMEM((128, D), BF16),
            pltpu.VMEM((2, PAIRS, 128, 256), F32),
            pltpu.VMEM((2, 128, HALF), BF16),
            pltpu.VMEM((128, HALF), BF16),
            pltpu.VMEM((HALF, 256), BF16),
            pltpu.VMEM((2, 2, SLOTS + 1, TOK, D), F32),
            pltpu.VMEM((2, 4, TOK, D), BF16),
            pltpu.VMEM((2, 4, TOK, D), BF16),
            pltpu.VMEM((2, 2, 2, TOK, D), BF16),
            pltpu.VMEM((2, 2, 2, TOK, D), BF16),
            pltpu.VMEM((2, 2, TOK, D), BF16),
            pltpu.VMEM((2, 2, TOK, D), BF16),
            pltpu.VMEM((FLAT, 128), BF16),
            pltpu.VMEM((GROUP, CHUNK, 128), BF16),
            pltpu.VMEM((CHUNK, 128), BF16),
            pltpu.VMEM((DEPTH, PIECE, 128), BF16),
            pltpu.VMEM((CHUNK, 128), BF16),
            pltpu.VMEM((2, FLAT, 128), BF16),
            dma((2, 8)),
            dma((2, 8)),
            dma((2,)),
            dma((2,)),
            dma((2,)),
            dma((2,)),
            dma((2, 2, 2)),
            dma((2, 2, 2)),
            dma((2,)),
            dma((2,)),
            dma((GROUP,)),
            dma((GROUP,)),
            dma((OWNERS,)),
            dma((DEPTH,)),
            dma((DEPTH,)),
            dma((OWNERS,)),
            dma((GROUP,)),
            dma((GROUP,)),
            dma((GROUP,)),
            dma((GROUP,)),
        ],
        compiler_params=pltpu.CompilerParams(
            collective_id=0, has_side_effects=True, vmem_limit_bytes=48 * 2**20
        ),
    )(
        queries.reshape(2, TOK, D),
        key_vectors.reshape(2, TOK, D),
        value_vectors.reshape(2, TOK, D),
        upstream.reshape(2 * TOK, D),
        w_out,
        neighbours,
        counts,
    )
    return (mixed.reshape(shape), dq.reshape(shape), dk.reshape(shape), dv.reshape(shape), wg)


def solution(mesh):
    grid = P("lat", "lon", None)
    return jax.shard_map(
        on_device,
        mesh=mesh,
        in_specs=(grid, grid, grid, grid, P(), P(), P()),
        out_specs=(grid, grid, grid, grid, P()),
        check_vma=False,
    )
```

time: 396 us -> 86.5 us (0.22)
  waiting for transfers between devices: 264 us -> 0 us
  Pallas kernels: 0 us -> 74.8 us
  local copies, waits for them, and re-layouts: 46.5 us -> 10.7 us
  other arithmetic: 34.4 us -> 0 us
  starting transfers between devices: 23.3 us -> 0 us
  between operations: 14.4 us -> 0.65 us
  matrix products: 11.4 us -> 0 us
    psum x1 -> x0, waiting for transfers between devices: 248 us -> none  [on_device(): w_grad = lax.psum(local_weight, ('lat', 'lon')) / math.sqrt(tokens_all)]
    pallas_call x0 -> x1, Pallas kernels: none -> 74.8 us  [on_device(): pl.pallas_call(kernel, out_shape=(jax.ShapeDtypeStruct((2 * TOK, D), BF16...]
    another operation x12 -> x0, local copies, waits for them, and re-layouts: 24.5 us -> none  [the longest x8 12.7 us: split_heads(): block_tiles.reshape(block_tiles.shape[0], block_tiles.shape[1], HEADS, HE...]
    ppermute x8 -> x0, starting transfers between devices: 23.3 us -> none  [the longest x4 12.9 us: padded_2(): after = lax.ppermute(leading, axis, down)]
    ppermute x8 -> x0, waiting for transfers between devices: 16.4 us -> none  [the longest x4 10.1 us: padded_2(): before = lax.ppermute(last, axis, up)]
    scatter-add x4 -> x0, other arithmetic: 12.5 us -> none  [the longest x2 10 us: add_into(): jnp.zeros((pad_count, BLK * BLK * feat_width), jnp.float32).at[flat_place]]
    dot_general x9 -> x0, matrix products: 11.4 us -> none  [the longest x1 2.88 us: on_device(): lax.dot_general(flat_att, flat_grad, (((0,), (0,)), ((), ())), preferred_...]
    transpose x6 -> x0, local copies, waits for them, and re-layouts: 8.83 us -> none  [the longest x2 8.45 us: contract_keys(): jnp.einsum('nhqk,nqhd->nkhd', weights_low, split_heads(block_tiles), pref...]
  transfers between devices with their start and end apart: 9 -> 0, of which waited for: 8 -> 0; matrix products, arithmetic and copies ran while one was open for 6% -> 0% of each run, Pallas kernels for 0% -> 0%
where the time goes in v1:
time: 86.5 us; the launch traced here: 86.1 us
  Pallas kernels  74.8 us (86%)
  local copies, waits for them, and re-layouts  10.7 us (12%)
    pallas_call x1, Pallas kernels, on_device(): pl.pallas_call(kernel, out_shape=(jax.ShapeDtypeStruct((2 * TOK, D), BF16...  74.8 us
    unnamed x18, local copies, waits for them, and re-layouts  10.7 us

profile of v1, /device:TPU:1, one launch (start us, length us, event | category | flops | bytes accessed | tf_op | source)
XLA Modules:
  0.0 86.1 jit_solution(16315383182229915872)
XLA Ops:
  0.6 0.9 %copy.12.nb_ref = s32[16,32,4]{2,1,0:T(8,128)S(1)} copy(s32[16,32,4]{1,2,0:T(4,128)} %param.12) | data formatting | bytes 16384 | tf_op args[5]
  1.6 0.0 copy-start
  1.6 1.3 %copy-done = bf16[768,768]{1,0:T(8,128)(2,1)S(1)} copy-done((bf16[768,768]{1,0:T(8,128)(2,1)S(1)}, bf16[768,768]{1,0:T(8,128)(2,1)}, u32[]{:S(2)}) %copy-start) | copy-done | bytes 1179672
  2.8 0.0 copy-start.1
  2.8 0.9 %copy-done.1 = bf16[16,8,768]{2,1,0:T(8,128)(2,1)S(1)} copy-done((bf16[16,8,768]{2,1,0:T(8,128)(2,1)S(1)}, bf16[16,8,768]{2,1,0:T(8,128)(2,1)}, u32[]{:S(2)}) %copy-start.1) | copy-done | bytes 196632
  3.8 0.0 copy-start.2
  3.8 0.9 %copy-done.2 = bf16[16,8,768]{2,1,0:T(8,128)(2,1)S(1)} copy-done((bf16[16,8,768]{2,1,0:T(8,128)(2,1)S(1)}, bf16[16,8,768]{2,1,0:T(8,128)(2,1)}, u32[]{:S(2)}) %copy-start.2) | copy-done | bytes 196632
  4.7 0.0 copy-start.3
  4.7 0.9 %copy-done.3 = bf16[16,8,768]{2,1,0:T(8,128)(2,1)S(1)} copy-done((bf16[16,8,768]{2,1,0:T(8,128)(2,1)S(1)}, bf16[16,8,768]{2,1,0:T(8,128)(2,1)}, u32[]{:S(2)}) %copy-start.3) | copy-done | bytes 196632
  5.6 0.0 copy-start.4
  5.6 0.9 %copy-done.4 = bf16[16,8,768]{2,1,0:T(8,128)(2,1)S(1)} copy-done((bf16[16,8,768]{2,1,0:T(8,128)(2,1)S(1)}, bf16[16,8,768]{2,1,0:T(8,128)(2,1)}, u32[]{:S(2)}) %copy-start.4) | copy-done | bytes 196632
  6.5 0.0 copy-start.5
  6.5 0.7 copy-done.5
  7.2 74.8 %shard_map.110 = (bf16[128,768]{1,0:T(8,128)(2,1)S(1)}, bf16[2,64,768]{2,1,0:T(8,128)(2,1)S(1)}, bf16[2,64,768]{2,1,0:T(8,128)(2,1)S(1)}, bf16[2,64,768]{2,1,0:T(8,128)(2,1)S(1)}, f32[768,768]{1,0:T(8,128)S(1)}) custom-call(bf16[2,64,768]{2,1,0:T(8,128)(2,1)S(1)} %bitcast.8, bf16[2,64,768]{2,1,0:T(8,128)(2,1)S(1)} %bitcast.9, ...), custom_call_target="tpu_custom_call" | custom-call | tf_op jit(solution)/shard_map/pallas_call | solution.py:525
  82.0 0.7 copy.18
  82.7 0.7 copy.19
  83.4 0.7 copy.20
  84.1 0.7 copy.21
  84.7 1.4 %copy.22 = f32[768,768]{1,0:T(8,128)} copy(f32[768,768]{1,0:T(8,128)S(1)} %get-tuple-element.24) | data formatting | bytes 4718592
Async XLA Ops:
  1.6 1.3 %copy-start = (bf16[768,768]{1,0:T(8,128)(2,1)S(1)}, bf16[768,768]{1,0:T(8,128)(2,1)}, u32[]{:S(2)}) copy-start(bf16[768,768]{1,0:T(8,128)(2,1)} %w_ref.1) | copy-start | bytes 3538948
  2.8 0.9 %copy-start.1 = (bf16[16,8,768]{2,1,0:T(8,128)(2,1)S(1)}, bf16[16,8,768]{2,1,0:T(8,128)(2,1)}, u32[]{:S(2)}) copy-start(bf16[16,8,768]{2,1,0:T(8,128)(2,1)} %param.7) | copy-start | bytes 589828
  3.8 0.9 %copy-start.2 = (bf16[16,8,768]{2,1,0:T(8,128)(2,1)S(1)}, bf16[16,8,768]{2,1,0:T(8,128)(2,1)}, u32[]{:S(2)}) copy-start(bf16[16,8,768]{2,1,0:T(8,128)(2,1)} %param.8) | copy-start | bytes 589828
  4.7 0.9 %copy-start.3 = (bf16[16,8,768]{2,1,0:T(8,128)(2,1)S(1)}, bf16[16,8,768]{2,1,0:T(8,128)(2,1)}, u32[]{:S(2)}) copy-start(bf16[16,8,768]{2,1,0:T(8,128)(2,1)} %param.9) | copy-start | bytes 589828
  5.6 0.9 %copy-start.4 = (bf16[16,8,768]{2,1,0:T(8,128)(2,1)S(1)}, bf16[16,8,768]{2,1,0:T(8,128)(2,1)}, u32[]{:S(2)}) copy-start(bf16[16,8,768]{2,1,0:T(8,128)(2,1)} %param.10) | copy-start | bytes 589828
  6.5 0.7 copy-start.5

commit v2 on v1

--- a/solution.py
+++ b/solution.py
@@ -26,6 +26,7 @@
 OWNERS = 3
 PIECE = CHUNK // OWNERS
 DEPTH = 8
+VMEM = 58 * 2**20
 NT = (((1,), (1,)), ((), ()))
 TN = (((0,), (0,)), ((), ()))
 
@@ -42,18 +43,27 @@
 
 
 def kernel(
-    q_ref,
-    k_ref,
-    v_ref,
-    u_ref,
-    w_ref,
-    nb_ref,
-    ct_ref,
+    q_hbm,
+    k_hbm,
+    v_hbm,
+    u_hbm,
+    w_hbm,
+    nb_hbm,
+    ct_hbm,
+    mixed_hbm,
+    dq_hbm,
+    dk_hbm,
+    dv_hbm,
+    wfin_hbm,
     mixed_ref,
     dq_ref,
     dk_ref,
     dv_ref,
-    wg_ref,
+    wfin,
+    q_ref,
+    w_ref,
+    nb_ref,
+    ct_ref,
     kvb,
     ucat,
     datt,
@@ -73,7 +83,8 @@
     zsum,
     zin,
     wch,
-    wfin,
+    in_s,
+    out_s,
     halo_s,
     halo_r,
     u_s,
@@ -133,15 +144,42 @@
     def _(k):
         greet(zpeer(lax.rem(z + k, DEPTH)))
 
-    kvb[0, 1, 1:3] = k_ref[...]
-    kvb[1, 1, 1:3] = v_ref[...]
-    ucat[0:128] = u_ref[...]
+    own_u = ucat.at[pl.ds(0, 128)]
+    loads = [
+        pltpu.make_async_copy(src, dst, in_s.at[i])
+        for i, (src, dst) in enumerate(
+            (
+                (u_hbm, own_u),
+                (w_hbm, w_ref),
+                (k_hbm, kvb.at[0, 1, pl.ds(1, 2)]),
+                (v_hbm, kvb.at[1, 1, pl.ds(1, 2)]),
+                (q_hbm, q_ref),
+                (nb_hbm, nb_ref),
+                (ct_hbm, ct_ref),
+            )
+        )
+    ]
+    for load in loads:
+        load.start()
     pl.semaphore_wait(barrier, 2 + GROUP - 1 + DEPTH - 1)
+
+    stores = [
+        pltpu.make_async_copy(src, dst, out_s.at[i])
+        for i, (src, dst) in enumerate(
+            (
+                (mixed_ref, mixed_hbm),
+                (dq_ref, dq_hbm),
+                (dk_ref, dk_hbm),
+                (dv_ref, dv_hbm),
+                (wfin, wfin_hbm),
+            )
+        )
+    ]
 
     def halo(t, i, src, dst, device):
         return remote(src, dst, halo_s.at[t, i], halo_r.at[t, i], device)
 
-    ins = (k_ref, v_ref)
+    ins = (k_hbm, v_hbm)
 
     def first(t):
         src = ins[t]
@@ -166,50 +204,54 @@
         pl.when(has_up)(c[1].start)
         pl.when(has_down)(c[2].start)
         c[3].start()
-    send_u = remote(u_ref, ucat.at[pl.ds(128, 128)], u_s.at[0], u_r.at[0], mate)
+    send_u = remote(u_hbm, ucat.at[pl.ds(128, 128)], u_s.at[0], u_r.at[0], mate)
     send_u.start()
 
+    loads[0].wait()
+    loads[1].wait()
     datt[...] = lax.dot_general(
-        u_ref[...], w_ref[...], NT, preferred_element_type=F32
+        own_u[...], w_ref[...], NT, preferred_element_type=F32
     ).astype(BF16)
     for t in range(2):
         for s in range(2):
             cb[t, s, SLOTS] = jnp.zeros((TOK, D), F32)
 
+    for load in loads[2:]:
+        load.wait()
     for t in range(2):
         c = second(t)
-        halo(t, 1, k_ref, kvb.at[t, oc, pl.ds(1, 2)], beyond).wait_recv()
+        halo(t, 1, k_hbm, kvb.at[t, oc, pl.ds(1, 2)], beyond).wait_recv()
         pl.when(has_up)(c[0].start)
         pl.when(has_down)(c[1].start)
 
         @pl.when(has_up)
         def _():
-            halo(t, 3, k_ref.at[0], kvb.at[t, 1, 0], up).wait_recv()
+            halo(t, 3, k_hbm.at[0], kvb.at[t, 1, 0], up).wait_recv()
             c[2].start()
 
         @pl.when(has_down)
         def _():
-            halo(t, 2, k_ref.at[0], kvb.at[t, 1, 3], down).wait_recv()
+            halo(t, 2, k_hbm.at[0], kvb.at[t, 1, 3], down).wait_recv()
             c[3].start()
 
     for t in range(2):
-        halo(t, 0, k_ref, kvb.at[t, ic, pl.ds(1, 2)], mate).wait_recv()
+        halo(t, 0, k_hbm, kvb.at[t, ic, pl.ds(1, 2)], mate).wait_recv()
 
         @pl.when(has_up)
         def _():
-            halo(t, 5, k_ref.at[0], kvb.at[t, oc, 0], up).wait_recv()
-            halo(t, 6, k_ref.at[0], kvb.at[t, ic, 0], mate).wait_recv()
+            halo(t, 5, k_hbm.at[0], kvb.at[t, oc, 0], up).wait_recv()
+            halo(t, 6, k_hbm.at[0], kvb.at[t, ic, 0], mate).wait_recv()
 
         @pl.when(has_down)
         def _():
-            halo(t, 4, k_ref.at[0], kvb.at[t, oc, 3], down).wait_recv()
-            halo(t, 7, k_ref.at[0], kvb.at[t, ic, 3], mate).wait_recv()
+            halo(t, 4, k_hbm.at[0], kvb.at[t, oc, 3], down).wait_recv()
+            halo(t, 7, k_hbm.at[0], kvb.at[t, ic, 3], mate).wait_recv()
 
     def places(s_block):
         i = 2 * a + s_block
         out = []
         for s in range(SLOTS):
-            name = nb_ref[i, b, s]
+            name = nb_ref[i, s, b]
             row = lax.div(name, NLON) - i + 1
             col = lax.rem(lax.rem(name, NLON) - b + 1 + NLON, NLON)
             out.append((jnp.clip(col, 0, 2), jnp.clip(row, 0, 2)))
@@ -261,7 +303,8 @@
     att_t[:, 0:128] = att2[core].T
     att = jnp.concatenate([att2[0], att2[1]], axis=1)
     mixed_ref[...] = jnp.dot(att, w_ref[...], preferred_element_type=F32).astype(BF16)
-    remote(u_ref, ucat.at[pl.ds(128, 128)], u_s.at[0], u_r.at[0], mate).wait_recv()
+    stores[0].start()
+    remote(u_hbm, ucat.at[pl.ds(128, 128)], u_s.at[0], u_r.at[0], mate).wait_recv()
     send_att.wait_recv()
     att_t[:, 128:256] = att_in[...].T
     for g in range(3):
@@ -306,6 +349,7 @@
                 cb[0, s, i, :, lanes] = dk[i * TOK : (i + 1) * TOK]
                 cb[1, s, i, :, lanes] = dv[i * TOK : (i + 1) * TOK]
 
+    stores[1].start()
     placed = [places(s) for s in range(2)]
 
     def slot_of(s, row, col):
@@ -459,6 +503,8 @@
                 x = terms(t, 1, 1 + r) + grp[t, 1 + r].astype(F32) + gro[t, r].astype(F32)
                 outs[t][r] = (x + grl[t, way, 1].astype(F32)).astype(BF16)
 
+        stores[2 + t].start()
+
     @pl.loop(1, GROUP)
     def _(k):
         m = lax.rem(n + GROUP - k, GROUP)
@@ -466,21 +512,11 @@
         remote(wch, wfin.at[core, chunk(m)], ag_s.at[k], ag_r.at[k], device).wait_recv()
         pass_on(k, core).start()
 
-    rows_of = pl.ds(pl.multiple_of(core * HALF, HALF), HALF)
-    for g in range(D // 128):
-        wg_ref[rows_of, g * 128 : g * 128 + 128] = wfin[
-            core, g * HALF : (g + 1) * HALF
-        ].astype(F32)
-
     @pl.loop(0, GROUP)
     def _(k):
         pass_on(k, 1 - core).wait_recv()
 
-    rows_of = pl.ds(pl.multiple_of((1 - core) * HALF, HALF), HALF)
-    for g in range(D // 128):
-        wg_ref[rows_of, g * 128 : g * 128 + 128] = wfin[
-            1 - core, g * HALF : (g + 1) * HALF
-        ].astype(F32)
+    stores[4].start()
 
     for t in range(2):
         c = first(t)
@@ -515,25 +551,57 @@
     def _(k):
         pass_on(k, core).wait_send()
 
+    for store in stores:
+        store.wait()
+
+
+def finish(mixed, dq, dk, dv, wfin, mixed_out, dq_out, dk_out, dv_out, wg_out, narrow, wide, sems):
+    large = [pltpu.make_async_copy(wfin.at[h], narrow.at[h], sems.at[h]) for h in range(2)]
+    small = [
+        pltpu.make_async_copy(src, dst, sems.at[2 + i])
+        for i, (src, dst) in enumerate(
+            ((mixed, mixed_out), (dq, dq_out), (dk, dk_out), (dv, dv_out))
+        )
+    ]
+    for copy in large + small:
+        copy.start()
+    for h in range(2):
+        rows = pl.ds(h * HALF, HALF)
+        large[h].wait()
+        for g in range(D // 128):
+            wide[rows, g * 128 : g * 128 + 128] = narrow[h, g * HALF : (g + 1) * HALF].astype(F32)
+        large.append(pltpu.make_async_copy(wide.at[rows], wg_out.at[rows], sems.at[6 + h]))
+        large[2 + h].start()
+    for copy in small + large[2:]:
+        copy.wait()
+
 
 def on_device(queries, key_vectors, value_vectors, upstream, w_out, neighbours, counts):
     shape = queries.shape
-    vmem = pl.BlockSpec(memory_space=pltpu.VMEM)
-    smem = pl.BlockSpec(memory_space=pltpu.SMEM)
+    hbm = pl.BlockSpec(memory_space=pltpu.HBM)
     blocks = jax.ShapeDtypeStruct((2, TOK, D), BF16)
     dma = pltpu.SemaphoreType.DMA
-    mixed, dq, dk, dv, wg = pl.pallas_call(
+    results = pl.pallas_call(
         kernel,
         out_shape=(
             jax.ShapeDtypeStruct((2 * TOK, D), BF16),
             blocks,
             blocks,
             blocks,
-            jax.ShapeDtypeStruct((D, D), F32),
+            jax.ShapeDtypeStruct((2, FLAT, 128), BF16),
         ),
-        in_specs=[vmem] * 5 + [smem] * 2,
-        out_specs=(vmem,) * 5,
+        in_specs=[hbm] * 7,
+        out_specs=(hbm,) * 5,
         scratch_shapes=[
+            pltpu.VMEM((2 * TOK, D), BF16),
+            pltpu.VMEM((2, TOK, D), BF16),
+            pltpu.VMEM((2, TOK, D), BF16),
+            pltpu.VMEM((2, TOK, D), BF16),
+            pltpu.VMEM((2, FLAT, 128), BF16),
+            pltpu.VMEM((2, TOK, D), BF16),
+            pltpu.VMEM((D, D), BF16),
+            pltpu.SMEM((16, SLOTS, NLON), jnp.int32),
+            pltpu.SMEM((16, NLON), jnp.int32),
             pltpu.VMEM((2, 3, 4, TOK, D), BF16),
             pltpu.VMEM((256, D), BF16),
             pltpu.VMEM((128, D), BF16),
@@ -553,7 +621,8 @@
             pltpu.VMEM((CHUNK, 128), BF16),
             pltpu.VMEM((DEPTH, PIECE, 128), BF16),
             pltpu.VMEM((CHUNK, 128), BF16),
-            pltpu.VMEM((2, FLAT, 128), BF16),
+            dma((7,)),
+            dma((5,)),
             dma((2, 8)),
             dma((2, 8)),
             dma((2,)),
@@ -576,7 +645,7 @@
             dma((GROUP,)),
         ],
         compiler_params=pltpu.CompilerParams(
-            collective_id=0, has_side_effects=True, vmem_limit_bytes=48 * 2**20
+            collective_id=0, has_side_effects=True, vmem_limit_bytes=VMEM
         ),
     )(
         queries.reshape(2, TOK, D),
@@ -584,9 +653,27 @@
         value_vectors.reshape(2, TOK, D),
         upstream.reshape(2 * TOK, D),
         w_out,
-        neighbours,
+        neighbours.transpose(0, 2, 1),
         counts,
     )
+    mixed, dq, dk, dv, wg = pl.pallas_call(
+        finish,
+        out_shape=(
+            jax.ShapeDtypeStruct((2 * TOK, D), BF16),
+            blocks,
+            blocks,
+            blocks,
+            jax.ShapeDtypeStruct((D, D), F32),
+        ),
+        in_specs=[hbm] * 5,
+        out_specs=(hbm,) * 5,
+        scratch_shapes=[
+            pltpu.VMEM((2, FLAT, 128), BF16),
+            pltpu.VMEM((D, D), F32),
+            dma((8,)),
+        ],
+        compiler_params=pltpu.CompilerParams(vmem_limit_bytes=VMEM),
+    )(*results)
     return (mixed.reshape(shape), dq.reshape(shape), dk.reshape(shape), dv.reshape(shape), wg)
 
 

time: 86.5 us -> 96.6 us (1.12)
  Pallas kernels: 74.8 us -> 95.9 us
  local copies, waits for them, and re-layouts: 10.7 us -> 0 us
    pallas_call x0 -> x1, Pallas kernels: none -> 25 us  [on_device(): pl.pallas_call(finish, out_shape=(jax.ShapeDtypeStruct((2 * TOK, D), BF16...]
    unnamed x18 -> x0, local copies, waits for them, and re-layouts: 10.7 us -> none
    pallas_call x1, Pallas kernels: 74.8 us -> 70.9 us  [on_device(): pl.pallas_call(kernel, out_shape=(jax.ShapeDtypeStruct((2 * TOK, D), BF16...]
where the time goes in v2:
time: 96.6 us; the launch traced here: 96.5 us
  Pallas kernels  95.9 us (99%)
    pallas_call x1, Pallas kernels, on_device(): pl.pallas_call(kernel, out_shape=(jax.ShapeDtypeStruct((2 * TOK, D), BF16...  70.9 us
    pallas_call x1, Pallas kernels, on_device(): pl.pallas_call(finish, out_shape=(jax.ShapeDtypeStruct((2 * TOK, D), BF16...  25 us

profile of v2, /device:TPU:1, one launch (start us, length us, event | category | flops | bytes accessed | tf_op | source)
XLA Modules:
  0.0 96.5 jit_solution(1361169621335936632)
XLA Ops:
  0.6 70.9 %shard_map.110 = (bf16[128,768]{1,0:T(8,128)(2,1)}, bf16[2,64,768]{2,1,0:T(8,128)(2,1)}, bf16[2,64,768]{2,1,0:T(8,128)(2,1)}, bf16[2,64,768]{2,1,0:T(8,128)(2,1)}, bf16[2,2304,128]{2,1,0:T(8,128)(2,1)}) custom-call(bf16[2,64,768]{2,1,0:T(8,128)(2,1)} %bitcast.9, bf16[2,64,768]{2,1,0:T(8,128)(2,1)} %bitcast.10, bf16[2,64,768]{2,1,0:T(8,128)(2,1)} %bitcast.11, ...), custom_call_target="tpu_custom_call" | custom-call | tf_op jit(solution)/shard_map/pallas_call | solution.py:584
  71.5 25.0 %shard_map.111 = (bf16[128,768]{1,0:T(8,128)(2,1)}, bf16[2,64,768]{2,1,0:T(8,128)(2,1)}, bf16[2,64,768]{2,1,0:T(8,128)(2,1)}, bf16[2,64,768]{2,1,0:T(8,128)(2,1)}, f32[768,768]{1,0:T(8,128)}) custom-call(bf16[128,768]{1,0:T(8,128)(2,1)} %get-tuple-element.15.mixed, bf16[2,64,768]{2,1,0:T(8,128)(2,1)} %get-tuple-element.16.dq, ...), custom_call_target="tpu_custom_call" | custom-call | tf_op jit(solution)/shard_map/pallas_call | solution.py:659

commit v3 on v2

--- a/solution.py
+++ b/solution.py
@@ -302,7 +302,9 @@
     send_att.start()
     att_t[:, 0:128] = att2[core].T
     att = jnp.concatenate([att2[0], att2[1]], axis=1)
-    mixed_ref[...] = jnp.dot(att, w_ref[...], preferred_element_type=F32).astype(BF16)
+    mixed = jnp.dot(att, w_ref[...], preferred_element_type=F32).astype(BF16)
+    mixed_ref[0] = mixed[:TOK]
+    mixed_ref[1] = mixed[TOK:]
     stores[0].start()
     remote(u_hbm, ucat.at[pl.ds(128, 128)], u_s.at[0], u_r.at[0], mate).wait_recv()
     send_att.wait_recv()
@@ -555,24 +557,28 @@
         store.wait()
 
 
-def finish(mixed, dq, dk, dv, wfin, mixed_out, dq_out, dk_out, dv_out, wg_out, narrow, wide, sems):
-    large = [pltpu.make_async_copy(wfin.at[h], narrow.at[h], sems.at[h]) for h in range(2)]
+def finish(mixed, dq, dk, dv, wfin, mixed_out, dq_out, dk_out, dv_out, wg_out, *scratch):
+    held, narrow, wide, in_s, out_s = scratch
+    large = [pltpu.make_async_copy(wfin.at[h], narrow.at[h], in_s.at[h]) for h in range(2)]
     small = [
-        pltpu.make_async_copy(src, dst, sems.at[2 + i])
-        for i, (src, dst) in enumerate(
-            ((mixed, mixed_out), (dq, dq_out), (dk, dk_out), (dv, dv_out))
-        )
+        pltpu.make_async_copy(src, held.at[i], in_s.at[2 + i])
+        for i, src in enumerate((mixed, dq, dk, dv))
     ]
     for copy in large + small:
         copy.start()
+    out = []
     for h in range(2):
         rows = pl.ds(h * HALF, HALF)
         large[h].wait()
         for g in range(D // 128):
             wide[rows, g * 128 : g * 128 + 128] = narrow[h, g * HALF : (g + 1) * HALF].astype(F32)
-        large.append(pltpu.make_async_copy(wide.at[rows], wg_out.at[rows], sems.at[6 + h]))
-        large[2 + h].start()
-    for copy in small + large[2:]:
+        out.append(pltpu.make_async_copy(wide.at[rows], wg_out.at[rows], out_s.at[h]))
+        out[h].start()
+    for i, dst in enumerate((mixed_out, dq_out, dk_out, dv_out)):
+        small[i].wait()
+        out.append(pltpu.make_async_copy(held.at[i], dst, out_s.at[2 + i]))
+        out[2 + i].start()
+    for copy in out:
         copy.wait()
 
 
@@ -584,7 +590,7 @@
     results = pl.pallas_call(
         kernel,
         out_shape=(
-            jax.ShapeDtypeStruct((2 * TOK, D), BF16),
+            blocks,
             blocks,
             blocks,
             blocks,
@@ -593,7 +599,7 @@
         in_specs=[hbm] * 7,
         out_specs=(hbm,) * 5,
         scratch_shapes=[
-            pltpu.VMEM((2 * TOK, D), BF16),
+            pltpu.VMEM((2, TOK, D), BF16),
             pltpu.VMEM((2, TOK, D), BF16),
             pltpu.VMEM((2, TOK, D), BF16),
             pltpu.VMEM((2, TOK, D), BF16),
@@ -659,7 +665,7 @@
     mixed, dq, dk, dv, wg = pl.pallas_call(
         finish,
         out_shape=(
-            jax.ShapeDtypeStruct((2 * TOK, D), BF16),
+            blocks,
             blocks,
             blocks,
             blocks,
@@ -668,9 +674,11 @@
         in_specs=[hbm] * 5,
         out_specs=(hbm,) * 5,
         scratch_shapes=[
+            pltpu.VMEM((4, 2, TOK, D), BF16),
             pltpu.VMEM((2, FLAT, 128), BF16),
             pltpu.VMEM((D, D), F32),
-            dma((8,)),
+            dma((6,)),
+            dma((6,)),
         ],
         compiler_params=pltpu.CompilerParams(vmem_limit_bytes=VMEM),
     )(*results)

time: 96.6 us -> 74.5 us (0.77)
  Pallas kernels: 95.9 us -> 73.7 us
    pallas_call x2, Pallas kernels: 95.9 us -> 73.7 us  [the longest x1 70.9 us: on_device(): pl.pallas_call(kernel, out_shape=(blocks, blocks, blocks, blocks, jax.Sha...]
where the time goes in v3:
time: 74.5 us; the launch traced here: 74.4 us
  Pallas kernels  73.7 us (99%)
    pallas_call x1, Pallas kernels, on_device(): pl.pallas_call(kernel, out_shape=(blocks, blocks, blocks, blocks, jax.Sha...  70.9 us
    pallas_call x1, Pallas kernels, on_device(): pl.pallas_call(finish, out_shape=(blocks, blocks, blocks, blocks, jax.Sha...  2.9 us

profile of v3, /device:TPU:1, one launch (start us, length us, event | category | flops | bytes accessed | tf_op | source)
XLA Modules:
  0.0 74.4 jit_solution(5467306175872570279)
XLA Ops:
  0.6 70.9 %shard_map.110 = (bf16[2,64,768]{2,1,0:T(8,128)(2,1)}, bf16[2,64,768]{2,1,0:T(8,128)(2,1)}, bf16[2,64,768]{2,1,0:T(8,128)(2,1)}, bf16[2,64,768]{2,1,0:T(8,128)(2,1)}, bf16[2,2304,128]{2,1,0:T(8,128)(2,1)}) custom-call(bf16[2,64,768]{2,1,0:T(8,128)(2,1)} %bitcast.9, bf16[2,64,768]{2,1,0:T(8,128)(2,1)} %bitcast.10, bf16[2,64,768]{2,1,0:T(8,128)(2,1)} %bitcast.11, ...), custom_call_target="tpu_custom_call" | custom-call | tf_op jit(solution)/shard_map/pallas_call | solution.py:590
  71.5 2.9 %shard_map.111 = (bf16[2,64,768]{2,1,0:T(8,128)(2,1)}, bf16[2,64,768]{2,1,0:T(8,128)(2,1)}, bf16[2,64,768]{2,1,0:T(8,128)(2,1)}, bf16[2,64,768]{2,1,0:T(8,128)(2,1)}, f32[768,768]{1,0:T(8,128)}) custom-call(bf16[2,64,768]{2,1,0:T(8,128)(2,1)} %get-tuple-element.15.mixed, bf16[2,64,768]{2,1,0:T(8,128)(2,1)} %get-tuple-element.16.dq, ...), custom_call_target="tpu_custom_call" | custom-call | tf_op jit(solution)/shard_map/pallas_call | solution.py:665

commit v4 on v3

--- a/solution.py
+++ b/solution.py
@@ -115,6 +115,8 @@
     has_down = a < NLAT - 1
     mate = (a, b + 1 - 2 * core)
     beyond = (a, lax.rem(b + NLON - 1 + 2 * core, NLON))
+    seam = (a == NLAT // 2, a == NLAT // 2 - 1)
+    near = (has_up & (a != NLAT // 2), has_down & (a != NLAT // 2 - 1))
     up = (a - 1, b)
     down = (a + 1, b)
     oc = 2 * core
@@ -196,6 +198,8 @@
             halo(t, 5, kvb.at[t, oc, 2], kvb.at[t, oc, 0], down),
             halo(t, 6, kvb.at[t, 1, 0], kvb.at[t, oc, 0], mate),
             halo(t, 7, kvb.at[t, 1, 3], kvb.at[t, oc, 3], mate),
+            remote(kvb.at[t, 1, 0], kvb.at[t, ic, 0], halo_s.at[t, 4], halo_r.at[t, 5], beyond),
+            remote(kvb.at[t, 1, 3], kvb.at[t, ic, 3], halo_s.at[t, 5], halo_r.at[t, 4], beyond),
         )
 
     for t in range(2):
@@ -221,17 +225,19 @@
     for t in range(2):
         c = second(t)
         halo(t, 1, k_hbm, kvb.at[t, oc, pl.ds(1, 2)], beyond).wait_recv()
-        pl.when(has_up)(c[0].start)
-        pl.when(has_down)(c[1].start)
+        pl.when(near[0])(c[0].start)
+        pl.when(near[1])(c[1].start)
 
         @pl.when(has_up)
         def _():
             halo(t, 3, k_hbm.at[0], kvb.at[t, 1, 0], up).wait_recv()
+            pl.when(seam[0])(c[4].start)
             c[2].start()
 
         @pl.when(has_down)
         def _():
             halo(t, 2, k_hbm.at[0], kvb.at[t, 1, 3], down).wait_recv()
+            pl.when(seam[1])(c[5].start)
             c[3].start()
 
     for t in range(2):
@@ -301,11 +307,6 @@
     send_att = remote(att2.at[1 - core], att_in, u_s.at[1], u_r.at[1], mate)
     send_att.start()
     att_t[:, 0:128] = att2[core].T
-    att = jnp.concatenate([att2[0], att2[1]], axis=1)
-    mixed = jnp.dot(att, w_ref[...], preferred_element_type=F32).astype(BF16)
-    mixed_ref[0] = mixed[:TOK]
-    mixed_ref[1] = mixed[TOK:]
-    stores[0].start()
     remote(u_hbm, ucat.at[pl.ds(128, 128)], u_s.at[0], u_r.at[0], mate).wait_recv()
     send_att.wait_recv()
     att_t[:, 128:256] = att_in[...].T
@@ -326,6 +327,12 @@
     @pl.loop(1, GROUP)
     def _(k):
         reduce_copy(k).start()
+
+    att = jnp.concatenate([att2[0], att2[1]], axis=1)
+    mixed = jnp.dot(att, w_ref[...], preferred_element_type=F32).astype(BF16)
+    mixed_ref[0] = mixed[:TOK]
+    mixed_ref[1] = mixed[TOK:]
+    stores[0].start()
 
     @pl.loop(0, 2)
     def _(s):
@@ -383,6 +390,15 @@
             device,
         )
 
+    def over_seam(t, way):
+        return remote(
+            gsl.at[t, way, 0],
+            grl.at[t, 1 - way, 0],
+            gl_s.at[t, way, 0],
+            gl_r.at[t, 1 - way, 0],
+            beyond,
+        )
+
     def to_beyond(t):
         return remote(gso.at[t], gro.at[t], go_s.at[t], go_r.at[t], beyond)
 
@@ -397,7 +413,9 @@
             @pl.when(conds[way])
             def _():
                 gsl[t, way, 0] = terms(t, oc, 3 * way).astype(BF16)
-                to_lat(t, way, 0).start()
+
+            pl.when(near[way])(to_lat(t, way, 0).start)
+            pl.when(seam[way])(over_seam(t, way).start)
 
     total = wbuf[chunk(n), :].astype(F32)
     for k in range(1, GROUP):
@@ -418,14 +436,36 @@
         pl.when(z != owner_z(o))(z_copy(o).start)
 
     for t in range(2):
+        for r in range(2):
+            x = terms(t, oc, 1 + r)
+            gso[t, r] = x.astype(BF16)
+        for way in range(2):
+
+            @pl.when(near[1 - way])
+            def _():
+                to_lat(t, way, 0).wait_recv()
+                r = 1 - way
+                x = terms(t, oc, 1 + r) + grl[t, way, 0].astype(F32)
+                gso[t, r] = x.astype(BF16)
+
+        to_beyond(t).start()
+
+    for t in range(2):
         to_mate(t).wait_recv()
         for way in range(2):
 
-            @pl.when(conds[way])
+            @pl.when(near[way])
             def _():
                 x = terms(t, 1, 3 * way) + grp[t, 3 * way].astype(F32)
                 gsl[t, way, 1] = x.astype(BF16)
-                to_lat(t, way, 1).start()
+
+            @pl.when(seam[way])
+            def _():
+                over_seam(t, way).wait_recv()
+                x = terms(t, 1, 3 * way) + grp[t, 3 * way].astype(F32)
+                gsl[t, way, 1] = (x + grl[t, 1 - way, 0].astype(F32)).astype(BF16)
+
+            pl.when(conds[way])(to_lat(t, way, 1).start)
 
     def z_gather(o, k):
         return remote(
@@ -453,21 +493,6 @@
             wch[o * PIECE : (o + 1) * PIECE] = (acc * (1.0 / math.sqrt(TOKENS))).astype(BF16)
             for k in range(1, DEPTH):
                 z_gather(o, k).start()
-
-    for t in range(2):
-        for r in range(2):
-            x = terms(t, oc, 1 + r)
-            gso[t, r] = x.astype(BF16)
-        for way in range(2):
-
-            @pl.when(from_conds[way])
-            def _():
-                to_lat(t, way, 0).wait_recv()
-                r = 1 - way
-                x = terms(t, oc, 1 + r) + grl[t, way, 0].astype(F32)
-                gso[t, r] = x.astype(BF16)
-
-        to_beyond(t).start()
 
     for o in range(OWNERS):
         pl.when(z != owner_z(o))(z_gather(o, 1).wait_recv)

time: 74.5 us -> 68.4 us (0.918)
  Pallas kernels: 73.7 us -> 67.6 us
    pallas_call x1, Pallas kernels: 70.9 us -> 64.8 us  [on_device(): pl.pallas_call(kernel, out_shape=(blocks, blocks, blocks, blocks, jax.Sha...]
where the time goes in v4:
time: 68.4 us; the launch traced here: 68.3 us
  Pallas kernels  67.6 us (99%)
    pallas_call x1, Pallas kernels, on_device(): pl.pallas_call(kernel, out_shape=(blocks, blocks, blocks, blocks, jax.Sha...  64.8 us
    pallas_call x1, Pallas kernels, on_device(): pl.pallas_call(finish, out_shape=(blocks, blocks, blocks, blocks, jax.Sha...  2.9 us

profile of v4, /device:TPU:1, one launch (start us, length us, event | category | flops | bytes accessed | tf_op | source)
XLA Modules:
  0.0 68.3 jit_solution(16558537190988980572)
XLA Ops:
  0.6 64.8 %shard_map.110 = (bf16[2,64,768]{2,1,0:T(8,128)(2,1)}, bf16[2,64,768]{2,1,0:T(8,128)(2,1)}, bf16[2,64,768]{2,1,0:T(8,128)(2,1)}, bf16[2,64,768]{2,1,0:T(8,128)(2,1)}, bf16[2,2304,128]{2,1,0:T(8,128)(2,1)}) custom-call(bf16[2,64,768]{2,1,0:T(8,128)(2,1)} %bitcast.9, bf16[2,64,768]{2,1,0:T(8,128)(2,1)} %bitcast.10, bf16[2,64,768]{2,1,0:T(8,128)(2,1)} %bitcast.11, ...), custom_call_target="tpu_custom_call" | custom-call | tf_op jit(solution)/shard_map/pallas_call | solution.py:615
  65.4 2.9 %shard_map.111 = (bf16[2,64,768]{2,1,0:T(8,128)(2,1)}, bf16[2,64,768]{2,1,0:T(8,128)(2,1)}, bf16[2,64,768]{2,1,0:T(8,128)(2,1)}, bf16[2,64,768]{2,1,0:T(8,128)(2,1)}, f32[768,768]{1,0:T(8,128)}) custom-call(bf16[2,64,768]{2,1,0:T(8,128)(2,1)} %get-tuple-element.15.mixed, bf16[2,64,768]{2,1,0:T(8,128)(2,1)} %get-tuple-element.16.dq, ...), custom_call_target="tpu_custom_call" | custom-call | tf_op jit(solution)/shard_map/pallas_call | solution.py:690

commit v5 on v4

--- a/solution.py
+++ b/solution.py
@@ -26,6 +26,10 @@
 OWNERS = 3
 PIECE = CHUNK // OWNERS
 DEPTH = 8
+STEPS = (
+    (2, 2), (2, 1), (2, 3), (1, 2), (3, 2), (1, 1), (3, 3), (1, 3), (3, 1), (2, 0), (0, 2), (1, 0),
+    (3, 0), (0, 1), (0, 3),
+)
 VMEM = 58 * 2**20
 NT = (((1,), (1,)), ((), ()))
 TN = (((0,), (0,)), ((), ()))
@@ -64,7 +68,8 @@
     w_ref,
     nb_ref,
     ct_ref,
-    kvb,
+    kb,
+    vb,
     ucat,
     datt,
     probs,
@@ -106,6 +111,7 @@
     fw_s,
     fw_r,
 ):
+    kvb = (kb, vb)
     a = lax.axis_index("lat")
     b = lax.axis_index("lon")
     core = lax.rem(b, 2)
@@ -121,11 +127,13 @@
     down = (a + 1, b)
     oc = 2 * core
     ic = 2 - oc
-    n = a * 2 + ylo
-
-    def peer(k):
-        m = lax.rem(n + k, GROUP)
-        return (m // 2, z * 4 + lax.rem(m, 2) * 2 + core), m
+    chip_x = lax.rem(a, 4)
+    chip_y = a // 4 * 2 + ylo
+    n = chip_x * 4 + chip_y
+
+    def peer(dx, dy):
+        px, py = lax.rem(chip_x + 4 + dx, 4), lax.rem(chip_y + 4 + dy, 4)
+        return (py // 2 * 4 + px, z * 4 + lax.rem(py, 2) * 2 + core), px * 4 + py
 
     def zpeer(zz):
         return (a, zz * 4 + ylo * 2 + core)
@@ -135,17 +143,12 @@
     def greet(device):
         pl.semaphore_signal(barrier, inc=1, device_id=device, device_id_type=MESH)
 
+    for k in (4, 3, 5, 2, 6, 1, 7):
+        greet(zpeer(lax.rem(z + k, DEPTH)))
+    for step in STEPS:
+        greet(peer(*step)[0])
+    greet(beyond)
     greet(mate)
-    greet(beyond)
-
-    @pl.loop(1, GROUP)
-    def _(k):
-        greet(peer(k)[0])
-
-    @pl.loop(1, DEPTH)
-    def _(k):
-        greet(zpeer(lax.rem(z + k, DEPTH)))
-
     own_u = ucat.at[pl.ds(0, 128)]
     loads = [
         pltpu.make_async_copy(src, dst, in_s.at[i])
@@ -153,8 +156,8 @@
             (
                 (u_hbm, own_u),
                 (w_hbm, w_ref),
-                (k_hbm, kvb.at[0, 1, pl.ds(1, 2)]),
-                (v_hbm, kvb.at[1, 1, pl.ds(1, 2)]),
+                (k_hbm, kvb[0].at[1, pl.ds(1, 2)]),
+                (v_hbm, kvb[1].at[1, pl.ds(1, 2)]),
                 (q_hbm, q_ref),
                 (nb_hbm, nb_ref),
                 (ct_hbm, ct_ref),
@@ -173,7 +176,6 @@
                 (dq_ref, dq_hbm),
                 (dk_ref, dk_hbm),
                 (dv_ref, dv_hbm),
-                (wfin, wfin_hbm),
             )
         )
     ]
@@ -186,28 +188,30 @@
     def first(t):
         src = ins[t]
         return (
-            halo(t, 1, src, kvb.at[t, ic, pl.ds(1, 2)], beyond),
-            halo(t, 2, src.at[0], kvb.at[t, 1, 3], up),
-            halo(t, 3, src.at[1], kvb.at[t, 1, 0], down),
-            halo(t, 0, src, kvb.at[t, oc, pl.ds(1, 2)], mate),
+            halo(t, 1, src.at[0], kvb[t].at[ic, 1], beyond),
+            halo(t, 8, src.at[1], kvb[t].at[ic, 2], beyond),
+            halo(t, 2, src.at[0], kvb[t].at[1, 3], up),
+            halo(t, 3, src.at[1], kvb[t].at[1, 0], down),
+            halo(t, 0, src, kvb[t].at[oc, pl.ds(1, 2)], mate),
         )
 
     def second(t):
         return (
-            halo(t, 4, kvb.at[t, oc, 1], kvb.at[t, oc, 3], up),
-            halo(t, 5, kvb.at[t, oc, 2], kvb.at[t, oc, 0], down),
-            halo(t, 6, kvb.at[t, 1, 0], kvb.at[t, oc, 0], mate),
-            halo(t, 7, kvb.at[t, 1, 3], kvb.at[t, oc, 3], mate),
-            remote(kvb.at[t, 1, 0], kvb.at[t, ic, 0], halo_s.at[t, 4], halo_r.at[t, 5], beyond),
-            remote(kvb.at[t, 1, 3], kvb.at[t, ic, 3], halo_s.at[t, 5], halo_r.at[t, 4], beyond),
+            halo(t, 4, kvb[t].at[oc, 1], kvb[t].at[oc, 3], up),
+            halo(t, 5, kvb[t].at[oc, 2], kvb[t].at[oc, 0], down),
+            halo(t, 6, kvb[t].at[1, 0], kvb[t].at[oc, 0], mate),
+            halo(t, 7, kvb[t].at[1, 3], kvb[t].at[oc, 3], mate),
+            remote(kvb[t].at[1, 0], kvb[t].at[ic, 0], halo_s.at[t, 4], halo_r.at[t, 5], beyond),
+            remote(kvb[t].at[1, 3], kvb[t].at[ic, 3], halo_s.at[t, 5], halo_r.at[t, 4], beyond),
         )
 
     for t in range(2):
         c = first(t)
         c[0].start()
-        pl.when(has_up)(c[1].start)
-        pl.when(has_down)(c[2].start)
-        c[3].start()
+        pl.when(has_up)(c[2].start)
+        c[1].start()
+        pl.when(has_down)(c[3].start)
+        c[4].start()
     send_u = remote(u_hbm, ucat.at[pl.ds(128, 128)], u_s.at[0], u_r.at[0], mate)
     send_u.start()
 
@@ -224,34 +228,36 @@
         load.wait()
     for t in range(2):
         c = second(t)
-        halo(t, 1, k_hbm, kvb.at[t, oc, pl.ds(1, 2)], beyond).wait_recv()
-        pl.when(near[0])(c[0].start)
-        pl.when(near[1])(c[1].start)
 
         @pl.when(has_up)
         def _():
-            halo(t, 3, k_hbm.at[0], kvb.at[t, 1, 0], up).wait_recv()
+            halo(t, 3, k_hbm.at[0], kvb[t].at[1, 0], up).wait_recv()
             pl.when(seam[0])(c[4].start)
             c[2].start()
 
         @pl.when(has_down)
         def _():
-            halo(t, 2, k_hbm.at[0], kvb.at[t, 1, 3], down).wait_recv()
+            halo(t, 2, k_hbm.at[0], kvb[t].at[1, 3], down).wait_recv()
             pl.when(seam[1])(c[5].start)
             c[3].start()
 
-    for t in range(2):
-        halo(t, 0, k_hbm, kvb.at[t, ic, pl.ds(1, 2)], mate).wait_recv()
+        halo(t, 1, k_hbm.at[0], kvb[t].at[oc, 1], beyond).wait_recv()
+        pl.when(near[0])(c[0].start)
+        halo(t, 8, k_hbm.at[0], kvb[t].at[oc, 2], beyond).wait_recv()
+        pl.when(near[1])(c[1].start)
+
+    def complete(t):
+        halo(t, 0, k_hbm, kvb[t].at[ic, pl.ds(1, 2)], mate).wait_recv()
 
         @pl.when(has_up)
         def _():
-            halo(t, 5, k_hbm.at[0], kvb.at[t, oc, 0], up).wait_recv()
-            halo(t, 6, k_hbm.at[0], kvb.at[t, ic, 0], mate).wait_recv()
+            halo(t, 6, k_hbm.at[0], kvb[t].at[ic, 0], mate).wait_recv()
+            halo(t, 5, k_hbm.at[0], kvb[t].at[oc, 0], up).wait_recv()
 
         @pl.when(has_down)
         def _():
-            halo(t, 4, k_hbm.at[0], kvb.at[t, oc, 3], down).wait_recv()
-            halo(t, 7, k_hbm.at[0], kvb.at[t, ic, 3], mate).wait_recv()
+            halo(t, 7, k_hbm.at[0], kvb[t].at[ic, 3], mate).wait_recv()
+            halo(t, 4, k_hbm.at[0], kvb[t].at[oc, 3], down).wait_recv()
 
     def places(s_block):
         i = 2 * a + s_block
@@ -265,7 +271,7 @@
 
     def blocks_of(t, place, s_block, j):
         return jnp.concatenate(
-            [kvb[t, col, row + s_block, :, pl.ds(j * 128, 128)] for col, row in place], axis=0
+            [kvb[t][col, row + s_block, :, pl.ds(j * 128, 128)] for col, row in place], axis=0
         )
 
     low = lax.broadcasted_iota(jnp.int32, (TOK, 128), 1) < HEAD_DIM
@@ -280,6 +286,118 @@
 
     def unstacked(x):
         return jnp.where(low, x[:TOK], x[TOK:])
+
+    placed = [places(s) for s in range(2)]
+
+    def slot_of(s, row, col):
+        slot = jnp.int32(SLOTS)
+        place, count = placed[s]
+        for i in range(SLOTS):
+            hit = (place[i][0] == col) & (place[i][1] == row) & (i < count)
+            slot = jnp.where(hit, i, slot)
+        return slot
+
+    def terms(t, col, row):
+        total = None
+        for s in range(2):
+            if 0 <= row - s <= 2:
+                x = cb[t, s, slot_of(s, row - s, col)]
+                total = x if total is None else total + x
+        return total
+
+    def to_mate(t):
+        return remote(gsp.at[t], grp.at[t], gp_s.at[t], gp_r.at[t], mate)
+
+    def to_lat(t, way, which):
+        device = (up, down)[way]
+        return remote(
+            gsl.at[t, way, which],
+            grl.at[t, way, which],
+            gl_s.at[t, way, which],
+            gl_r.at[t, way, which],
+            device,
+        )
+
+    def over_seam(t, way):
+        return remote(
+            gsl.at[t, way, 0],
+            grl.at[t, 1 - way, 0],
+            gl_s.at[t, way, 0],
+            gl_r.at[t, 1 - way, 0],
+            beyond,
+        )
+
+    def to_beyond(t):
+        return remote(gso.at[t], gro.at[t], go_s.at[t], go_r.at[t], beyond)
+
+    conds = (has_up, has_down)
+
+    def send_outer(t):
+        for way in range(2):
+
+            @pl.when(conds[way])
+            def _():
+                gsl[t, way, 0] = terms(t, oc, 3 * way).astype(BF16)
+
+            pl.when(near[way])(to_lat(t, way, 0).start)
+            pl.when(seam[way])(over_seam(t, way).start)
+
+    def send_mate(t):
+        for r in range(4):
+            gsp[t, r] = terms(t, ic, r).astype(BF16)
+        to_mate(t).start()
+
+    def send_beyond(t):
+        for r in range(2):
+
+            @pl.when(near[r])
+            def _():
+                to_lat(t, 1 - r, 0).wait_recv()
+                gso[t, r] = (terms(t, oc, 1 + r) + grl[t, 1 - r, 0].astype(F32)).astype(BF16)
+
+            @pl.when(jnp.logical_not(near[r]))
+            def _():
+                gso[t, r] = terms(t, oc, 1 + r).astype(BF16)
+
+        to_beyond(t).start()
+
+    def send_own(t):
+        to_mate(t).wait_recv()
+        for way in range(2):
+
+            @pl.when(near[way])
+            def _():
+                total = terms(t, 1, 3 * way) + grp[t, 3 * way].astype(F32)
+                gsl[t, way, 1] = total.astype(BF16)
+
+            @pl.when(seam[way])
+            def _():
+                over_seam(t, way).wait_recv()
+                total = terms(t, 1, 3 * way) + grp[t, 3 * way].astype(F32)
+                gsl[t, way, 1] = (total + grl[t, 1 - way, 0].astype(F32)).astype(BF16)
+
+            pl.when(conds[way])(to_lat(t, way, 1).start)
+
+    def final(t):
+        out = (dk_ref, dv_ref)[t]
+        to_beyond(t).wait_recv()
+        for r in range(2):
+
+            def total():
+                return terms(t, 1, 1 + r) + grp[t, 1 + r].astype(F32) + gro[t, r].astype(F32)
+
+            @pl.when(conds[r])
+            def _():
+                to_lat(t, 1 - r, 1).wait_recv()
+                out[r] = (total() + grl[t, 1 - r, 1].astype(F32)).astype(BF16)
+
+            @pl.when(jnp.logical_not(conds[r]))
+            def _():
+                out[r] = total().astype(BF16)
+
+        stores[2 + t].start()
+
+    complete(0)
 
     @pl.loop(0, 2)
     def _(s):
@@ -299,6 +417,25 @@
             e = jnp.exp(masked - top)
             probs[s, j] = e * (1.0 / jnp.sum(e, axis=-1, keepdims=True))
         for j in range(PAIRS):
+            lanes = pl.ds(j * 128, 128)
+            dv = lax.dot_general(
+                probs[s, j].astype(BF16),
+                stacked(datt[rows, lanes]),
+                TN,
+                preferred_element_type=F32,
+            )
+            for i in range(SLOTS):
+                cb[1, s, i, :, lanes] = dv[i * TOK : (i + 1) * TOK]
+
+    send_outer(1)
+    send_mate(1)
+    complete(1)
+
+    @pl.loop(0, 2)
+    def _(s):
+        place, _ = places(s)
+        rows = pl.ds(pl.multiple_of(s * TOK, TOK), TOK)
+        for j in range(PAIRS):
             o = jnp.dot(
                 probs[s, j].astype(BF16), blocks_of(1, place, s, j), preferred_element_type=F32
             )
@@ -307,6 +444,7 @@
     send_att = remote(att2.at[1 - core], att_in, u_s.at[1], u_r.at[1], mate)
     send_att.start()
     att_t[:, 0:128] = att2[core].T
+    send_beyond(1)
     remote(u_hbm, ucat.at[pl.ds(128, 128)], u_s.at[0], u_r.at[0], mate).wait_recv()
     send_att.wait_recv()
     att_t[:, 128:256] = att_in[...].T
@@ -321,11 +459,10 @@
         return pl.ds(pl.multiple_of(m * CHUNK, 16), CHUNK)
 
     def reduce_copy(k):
-        device, m = peer(k)
+        device, m = peer(*STEPS[k])
         return remote(wbuf.at[chunk(m)], rsin.at[k], rs_s.at[k], rs_r.at[k], device)
 
-    @pl.loop(1, GROUP)
-    def _(k):
+    for k in range(GROUP - 1):
         reduce_copy(k).start()
 
     att = jnp.concatenate([att2[0], att2[1]], axis=1)
@@ -333,6 +470,7 @@
     mixed_ref[0] = mixed[:TOK]
     mixed_ref[1] = mixed[TOK:]
     stores[0].start()
+    send_own(1)
 
     @pl.loop(0, 2)
     def _(s):
@@ -353,72 +491,15 @@
             dq = unstacked(jnp.dot(ds, ks, preferred_element_type=F32)) * 0.125
             dq_ref[s, :, lanes] = dq.astype(BF16)
             dk = lax.dot_general(ds, qs, TN, preferred_element_type=F32)
-            dv = lax.dot_general(p.astype(BF16), da, TN, preferred_element_type=F32)
             for i in range(SLOTS):
                 cb[0, s, i, :, lanes] = dk[i * TOK : (i + 1) * TOK]
-                cb[1, s, i, :, lanes] = dv[i * TOK : (i + 1) * TOK]
 
     stores[1].start()
-    placed = [places(s) for s in range(2)]
-
-    def slot_of(s, row, col):
-        slot = jnp.int32(SLOTS)
-        place, count = placed[s]
-        for i in range(SLOTS):
-            hit = (place[i][0] == col) & (place[i][1] == row) & (i < count)
-            slot = jnp.where(hit, i, slot)
-        return slot
-
-    def terms(t, col, row):
-        total = None
-        for s in range(2):
-            if 0 <= row - s <= 2:
-                x = cb[t, s, slot_of(s, row - s, col)]
-                total = x if total is None else total + x
-        return total
-
-    def to_mate(t):
-        return remote(gsp.at[t], grp.at[t], gp_s.at[t], gp_r.at[t], mate)
-
-    def to_lat(t, way, which):
-        device = (up, down)[way]
-        return remote(
-            gsl.at[t, way, which],
-            grl.at[t, way, which],
-            gl_s.at[t, way, which],
-            gl_r.at[t, way, which],
-            device,
-        )
-
-    def over_seam(t, way):
-        return remote(
-            gsl.at[t, way, 0],
-            grl.at[t, 1 - way, 0],
-            gl_s.at[t, way, 0],
-            gl_r.at[t, 1 - way, 0],
-            beyond,
-        )
-
-    def to_beyond(t):
-        return remote(gso.at[t], gro.at[t], go_s.at[t], go_r.at[t], beyond)
-
-    conds = (has_up, has_down)
-    from_conds = (has_down, has_up)
-    for t in range(2):
-        for r in range(4):
-            gsp[t, r] = terms(t, ic, r).astype(BF16)
-        to_mate(t).start()
-        for way in range(2):
-
-            @pl.when(conds[way])
-            def _():
-                gsl[t, way, 0] = terms(t, oc, 3 * way).astype(BF16)
-
-            pl.when(near[way])(to_lat(t, way, 0).start)
-            pl.when(seam[way])(over_seam(t, way).start)
+    send_outer(0)
+    send_mate(0)
 
     total = wbuf[chunk(n), :].astype(F32)
-    for k in range(1, GROUP):
+    for k in reversed(range(GROUP - 1)):
         reduce_copy(k).wait_recv()
         total = total + rsin[k].astype(F32)
     zsum[...] = total.astype(BF16)
@@ -434,38 +515,8 @@
 
     for o in range(OWNERS):
         pl.when(z != owner_z(o))(z_copy(o).start)
-
-    for t in range(2):
-        for r in range(2):
-            x = terms(t, oc, 1 + r)
-            gso[t, r] = x.astype(BF16)
-        for way in range(2):
-
-            @pl.when(near[1 - way])
-            def _():
-                to_lat(t, way, 0).wait_recv()
-                r = 1 - way
-                x = terms(t, oc, 1 + r) + grl[t, way, 0].astype(F32)
-                gso[t, r] = x.astype(BF16)
-
-        to_beyond(t).start()
-
-    for t in range(2):
-        to_mate(t).wait_recv()
-        for way in range(2):
-
-            @pl.when(near[way])
-            def _():
-                x = terms(t, 1, 3 * way) + grp[t, 3 * way].astype(F32)
-                gsl[t, way, 1] = x.astype(BF16)
-
-            @pl.when(seam[way])
-            def _():
-                over_seam(t, way).wait_recv()
-                x = terms(t, 1, 3 * way) + grp[t, 3 * way].astype(F32)
-                gsl[t, way, 1] = (x + grl[t, 1 - way, 0].astype(F32)).astype(BF16)
-
-            pl.when(conds[way])(to_lat(t, way, 1).start)
+    send_beyond(0)
+    send_own(0)
 
     def z_gather(o, k):
         return remote(
@@ -494,66 +545,41 @@
             for k in range(1, DEPTH):
                 z_gather(o, k).start()
 
+    final(1)
     for o in range(OWNERS):
         pl.when(z != owner_z(o))(z_gather(o, 1).wait_recv)
 
     def gather_copy(k):
-        device, _ = peer(k)
+        device, _ = peer(*STEPS[k])
         return remote(wch, wfin.at[core, chunk(n)], ag_s.at[k], ag_r.at[k], device)
 
-    @pl.loop(1, GROUP)
-    def _(k):
+    for k in range(GROUP - 1):
         gather_copy(k).start()
-
     wfin[core, chunk(n), :] = wch[...]
 
+    def source(k):
+        dx, dy = STEPS[k] if k < GROUP - 1 else (0, 0)
+        return peer(-dx, -dy)
+
     def pass_on(k, half):
-        m = lax.rem(n + GROUP - k, GROUP)
+        _, m = source(k)
         return remote(
             wfin.at[half, chunk(m)], wfin.at[half, chunk(m)], fw_s.at[k], fw_r.at[k], mate
         )
 
-    pass_on(0, core).start()
-
-    outs = (dk_ref, dv_ref)
-    for t in range(2):
-        to_beyond(t).wait_recv()
-        for r in range(2):
-            x = terms(t, 1, 1 + r) + grp[t, 1 + r].astype(F32) + gro[t, r].astype(F32)
-            outs[t][r] = x.astype(BF16)
-        for way in range(2):
-
-            @pl.when(from_conds[way])
-            def _():
-                to_lat(t, way, 1).wait_recv()
-                r = 1 - way
-                x = terms(t, 1, 1 + r) + grp[t, 1 + r].astype(F32) + gro[t, r].astype(F32)
-                outs[t][r] = (x + grl[t, way, 1].astype(F32)).astype(BF16)
-
-        stores[2 + t].start()
-
-    @pl.loop(1, GROUP)
-    def _(k):
-        m = lax.rem(n + GROUP - k, GROUP)
-        device = (m // 2, z * 4 + lax.rem(m, 2) * 2 + core)
-        remote(wch, wfin.at[core, chunk(m)], ag_s.at[k], ag_r.at[k], device).wait_recv()
-        pass_on(k, core).start()
-
-    @pl.loop(0, GROUP)
-    def _(k):
-        pass_on(k, 1 - core).wait_recv()
-
-    stores[4].start()
+    pass_on(GROUP - 1, core).start()
+
+    final(0)
 
     for t in range(2):
         c = first(t)
-        c[0].wait_send()
-        c[3].wait_send()
+        for i in (0, 1, 4):
+            c[i].wait_send()
         d = second(t)
-        for x in (c[1], d[0], d[2]):
-            pl.when(has_up)(x.wait_send)
-        for x in (c[2], d[1], d[3]):
-            pl.when(has_down)(x.wait_send)
+        for i in (c[2], d[0], d[2]):
+            pl.when(has_up)(i.wait_send)
+        for i in (c[3], d[1], d[3]):
+            pl.when(has_down)(i.wait_send)
         to_mate(t).wait_send()
         to_beyond(t).wait_send()
         for way in range(2):
@@ -569,17 +595,29 @@
             for k in range(1, DEPTH):
                 z_gather(o, k).wait_send()
 
-    @pl.loop(1, GROUP)
-    def _(k):
+    for k in range(GROUP - 1):
         reduce_copy(k).wait_send()
-        gather_copy(k).wait_send()
-
-    @pl.loop(0, GROUP)
-    def _(k):
-        pass_on(k, core).wait_send()
-
     for store in stores:
         store.wait()
+
+    for k in reversed(range(GROUP - 1)):
+        device, m = source(k)
+        remote(wch, wfin.at[core, chunk(m)], ag_s.at[k], ag_r.at[k], device).wait_recv()
+        pass_on(k, core).start()
+    halves = [
+        pltpu.make_async_copy(wfin.at[h], wfin_hbm.at[h], out_s.at[4 + i])
+        for i, h in enumerate((core, 1 - core))
+    ]
+    halves[0].start()
+    for k in reversed(range(GROUP)):
+        pass_on(k, 1 - core).wait_recv()
+    halves[1].start()
+    for k in range(GROUP - 1):
+        gather_copy(k).wait_send()
+    for k in range(GROUP):
+        pass_on(k, core).wait_send()
+    for half in halves:
+        half.wait()
 
 
 def finish(mixed, dq, dk, dv, wfin, mixed_out, dq_out, dk_out, dv_out, wg_out, *scratch):
@@ -633,7 +671,8 @@
             pltpu.VMEM((D, D), BF16),
             pltpu.SMEM((16, SLOTS, NLON), jnp.int32),
             pltpu.SMEM((16, NLON), jnp.int32),
-            pltpu.VMEM((2, 3, 4, TOK, D), BF16),
+            pltpu.VMEM((3, 4, TOK, D), BF16),
+            pltpu.VMEM((3, 4, TOK, D), BF16),
             pltpu.VMEM((256, D), BF16),
             pltpu.VMEM((128, D), BF16),
             pltpu.VMEM((2, PAIRS, 128, 256), F32),
@@ -648,14 +687,14 @@
             pltpu.VMEM((2, 2, TOK, D), BF16),
             pltpu.VMEM((2, 2, TOK, D), BF16),
             pltpu.VMEM((FLAT, 128), BF16),
-            pltpu.VMEM((GROUP, CHUNK, 128), BF16),
+            pltpu.VMEM((GROUP - 1, CHUNK, 128), BF16),
             pltpu.VMEM((CHUNK, 128), BF16),
             pltpu.VMEM((DEPTH, PIECE, 128), BF16),
             pltpu.VMEM((CHUNK, 128), BF16),
             dma((7,)),
-            dma((5,)),
-            dma((2, 8)),
-            dma((2, 8)),
+            dma((6,)),
+            dma((2, 9)),
+            dma((2, 9)),
             dma((2,)),
             dma((2,)),
             dma((2,)),

time: 68.4 us -> 65.9 us (0.963)
  Pallas kernels: 67.6 us -> 65.1 us
    pallas_call x1, Pallas kernels: 64.8 us -> 62.2 us  [on_device(): pl.pallas_call(kernel, out_shape=(blocks, blocks, blocks, blocks, jax.Sha...]
where the time goes in v5:
time: 65.9 us; the launch traced here: 65.8 us
  Pallas kernels  65.1 us (99%)
    pallas_call x1, Pallas kernels, on_device(): pl.pallas_call(kernel, out_shape=(blocks, blocks, blocks, blocks, jax.Sha...  62.2 us
    pallas_call x1, Pallas kernels, on_device(): pl.pallas_call(finish, out_shape=(blocks, blocks, blocks, blocks, jax.Sha...  2.9 us

profile of v5, /device:TPU:1, one launch (start us, length us, event | category | flops | bytes accessed | tf_op | source)
XLA Modules:
  0.0 65.8 jit_solution(1751500856475363829)
XLA Ops:
  0.6 62.2 %shard_map.110 = (bf16[2,64,768]{2,1,0:T(8,128)(2,1)}, bf16[2,64,768]{2,1,0:T(8,128)(2,1)}, bf16[2,64,768]{2,1,0:T(8,128)(2,1)}, bf16[2,64,768]{2,1,0:T(8,128)(2,1)}, bf16[2,2304,128]{2,1,0:T(8,128)(2,1)}) custom-call(bf16[2,64,768]{2,1,0:T(8,128)(2,1)} %bitcast.9, bf16[2,64,768]{2,1,0:T(8,128)(2,1)} %bitcast.10, bf16[2,64,768]{2,1,0:T(8,128)(2,1)} %bitcast.11, ...), custom_call_target="tpu_custom_call" | custom-call | tf_op jit(solution)/shard_map/pallas_call | solution.py:653
  62.9 2.9 %shard_map.111 = (bf16[2,64,768]{2,1,0:T(8,128)(2,1)}, bf16[2,64,768]{2,1,0:T(8,128)(2,1)}, bf16[2,64,768]{2,1,0:T(8,128)(2,1)}, bf16[2,64,768]{2,1,0:T(8,128)(2,1)}, f32[768,768]{1,0:T(8,128)}) custom-call(bf16[2,64,768]{2,1,0:T(8,128)(2,1)} %get-tuple-element.15.mixed, bf16[2,64,768]{2,1,0:T(8,128)(2,1)} %get-tuple-element.16.dq, ...), custom_call_target="tpu_custom_call" | custom-call | tf_op jit(solution)/shard_map/pallas_call | solution.py:729

commit v6 on v5

--- a/solution.py
+++ b/solution.py
@@ -431,6 +431,12 @@
     send_mate(1)
     complete(1)
 
+    def send_att(s):
+        rows = pl.ds(pl.multiple_of(s * TOK, TOK), TOK)
+        return remote(
+            att2.at[1 - core, rows], att_in.at[rows], u_s.at[1 + s], u_r.at[1 + s], mate
+        )
+
     @pl.loop(0, 2)
     def _(s):
         place, _ = places(s)
@@ -440,13 +446,12 @@
                 probs[s, j].astype(BF16), blocks_of(1, place, s, j), preferred_element_type=F32
             )
             att2[j // 3, rows, (j % 3) * 128 : (j % 3) * 128 + 128] = unstacked(o).astype(BF16)
-
-    send_att = remote(att2.at[1 - core], att_in, u_s.at[1], u_r.at[1], mate)
-    send_att.start()
+        send_att(s).start()
+
     att_t[:, 0:128] = att2[core].T
-    send_beyond(1)
     remote(u_hbm, ucat.at[pl.ds(128, 128)], u_s.at[0], u_r.at[0], mate).wait_recv()
-    send_att.wait_recv()
+    for s in range(2):
+        send_att(s).wait_recv()
     att_t[:, 128:256] = att_in[...].T
     for g in range(3):
         term = jnp.dot(
@@ -470,6 +475,7 @@
     mixed_ref[0] = mixed[:TOK]
     mixed_ref[1] = mixed[TOK:]
     stores[0].start()
+    send_beyond(1)
     send_own(1)
 
     @pl.loop(0, 2)
@@ -586,7 +592,8 @@
             for which in range(2):
                 pl.when(conds[way])(to_lat(t, way, which).wait_send)
     send_u.wait_send()
-    send_att.wait_send()
+    for s in range(2):
+        send_att(s).wait_send()
     for o in range(OWNERS):
         pl.when(z != owner_z(o))(z_copy(o).wait_send)
 
@@ -695,8 +702,8 @@
             dma((6,)),
             dma((2, 9)),
             dma((2, 9)),
-            dma((2,)),
-            dma((2,)),
+            dma((3,)),
+            dma((3,)),
             dma((2,)),
             dma((2,)),
             dma((2, 2, 2)),

time: 65.9 us -> 65 us (0.986)
  Pallas kernels: 65.1 us -> 64.2 us
    pallas_call x1, Pallas kernels: 62.2 us -> 61.3 us  [on_device(): pl.pallas_call(kernel, out_shape=(blocks, blocks, blocks, blocks, jax.Sha...]
where the time goes in v6:
time: 65 us; the launch traced here: 64.9 us
  Pallas kernels  64.2 us (99%)
    pallas_call x1, Pallas kernels, on_device(): pl.pallas_call(kernel, out_shape=(blocks, blocks, blocks, blocks, jax.Sha...  61.3 us
    pallas_call x1, Pallas kernels, on_device(): pl.pallas_call(finish, out_shape=(blocks, blocks, blocks, blocks, jax.Sha...  2.9 us

profile of v6, /device:TPU:1, one launch (start us, length us, event | category | flops | bytes accessed | tf_op | source)
XLA Modules:
  0.0 64.9 jit_solution(13703026687452911600)
XLA Ops:
  0.6 61.3 %shard_map.110 = (bf16[2,64,768]{2,1,0:T(8,128)(2,1)}, bf16[2,64,768]{2,1,0:T(8,128)(2,1)}, bf16[2,64,768]{2,1,0:T(8,128)(2,1)}, bf16[2,64,768]{2,1,0:T(8,128)(2,1)}, bf16[2,2304,128]{2,1,0:T(8,128)(2,1)}) custom-call(bf16[2,64,768]{2,1,0:T(8,128)(2,1)} %bitcast.9, bf16[2,64,768]{2,1,0:T(8,128)(2,1)} %bitcast.10, bf16[2,64,768]{2,1,0:T(8,128)(2,1)} %bitcast.11, ...), custom_call_target="tpu_custom_call" | custom-call | tf_op jit(solution)/shard_map/pallas_call | solution.py:660
  62.0 2.9 %shard_map.111 = (bf16[2,64,768]{2,1,0:T(8,128)(2,1)}, bf16[2,64,768]{2,1,0:T(8,128)(2,1)}, bf16[2,64,768]{2,1,0:T(8,128)(2,1)}, bf16[2,64,768]{2,1,0:T(8,128)(2,1)}, f32[768,768]{1,0:T(8,128)}) custom-call(bf16[2,64,768]{2,1,0:T(8,128)(2,1)} %get-tuple-element.15.mixed, bf16[2,64,768]{2,1,0:T(8,128)(2,1)} %get-tuple-element.16.dq, ...), custom_call_target="tpu_custom_call" | custom-call | tf_op jit(solution)/shard_map/pallas_call | solution.py:736

commit v7 on v6

--- a/solution.py
+++ b/solution.py
@@ -143,12 +143,6 @@
     def greet(device):
         pl.semaphore_signal(barrier, inc=1, device_id=device, device_id_type=MESH)
 
-    for k in (4, 3, 5, 2, 6, 1, 7):
-        greet(zpeer(lax.rem(z + k, DEPTH)))
-    for step in STEPS:
-        greet(peer(*step)[0])
-    greet(beyond)
-    greet(mate)
     own_u = ucat.at[pl.ds(0, 128)]
     loads = [
         pltpu.make_async_copy(src, dst, in_s.at[i])
@@ -166,7 +160,20 @@
     ]
     for load in loads:
         load.start()
-    pl.semaphore_wait(barrier, 2 + GROUP - 1 + DEPTH - 1)
+
+    is_owner = lax.rem(z, 3) == 0
+    for k in (4, 3, 5, 2, 6, 1, 7):
+        other = lax.rem(z + k, DEPTH)
+
+        @pl.when(is_owner | (lax.rem(other, 3) == 0))
+        def _():
+            greet(zpeer(other))
+
+    for step in STEPS:
+        greet(peer(*step)[0])
+    greet(beyond)
+    greet(mate)
+    pl.semaphore_wait(barrier, 2 + GROUP - 1 + jnp.where(is_owner, DEPTH - 1, OWNERS))
 
     stores = [
         pltpu.make_async_copy(src, dst, out_s.at[i])
@@ -470,11 +477,6 @@
     for k in range(GROUP - 1):
         reduce_copy(k).start()
 
-    att = jnp.concatenate([att2[0], att2[1]], axis=1)
-    mixed = jnp.dot(att, w_ref[...], preferred_element_type=F32).astype(BF16)
-    mixed_ref[0] = mixed[:TOK]
-    mixed_ref[1] = mixed[TOK:]
-    stores[0].start()
     send_beyond(1)
     send_own(1)
 
@@ -575,6 +577,11 @@
 
     pass_on(GROUP - 1, core).start()
 
+    att = jnp.concatenate([att2[0], att2[1]], axis=1)
+    mixed = jnp.dot(att, w_ref[...], preferred_element_type=F32).astype(BF16)
+    mixed_ref[0] = mixed[:TOK]
+    mixed_ref[1] = mixed[TOK:]
+    stores[0].start()
     final(0)
 
     for t in range(2):

time: 65 us -> 64.7 us (level)
  no operation moved by 1% of the time
where the time goes in v7:
time: 64.7 us; the launch traced here: 64.6 us
  Pallas kernels  63.9 us (99%)
    pallas_call x1, Pallas kernels, on_device(): pl.pallas_call(kernel, out_shape=(blocks, blocks, blocks, blocks, jax.Sha...  61 us
    pallas_call x1, Pallas kernels, on_device(): pl.pallas_call(finish, out_shape=(blocks, blocks, blocks, blocks, jax.Sha...  2.9 us

profile of v7, /device:TPU:1, one launch (start us, length us, event | category | flops | bytes accessed | tf_op | source)
XLA Modules:
  0.0 64.6 jit_solution(4423174763240958800)
XLA Ops:
  0.6 61.0 %shard_map.110 = (bf16[2,64,768]{2,1,0:T(8,128)(2,1)}, bf16[2,64,768]{2,1,0:T(8,128)(2,1)}, bf16[2,64,768]{2,1,0:T(8,128)(2,1)}, bf16[2,64,768]{2,1,0:T(8,128)(2,1)}, bf16[2,2304,128]{2,1,0:T(8,128)(2,1)}) custom-call(bf16[2,64,768]{2,1,0:T(8,128)(2,1)} %bitcast.9, bf16[2,64,768]{2,1,0:T(8,128)(2,1)} %bitcast.10, bf16[2,64,768]{2,1,0:T(8,128)(2,1)} %bitcast.11, ...), custom_call_target="tpu_custom_call" | custom-call | tf_op jit(solution)/shard_map/pallas_call | solution.py:667
  61.7 2.9 %shard_map.111 = (bf16[2,64,768]{2,1,0:T(8,128)(2,1)}, bf16[2,64,768]{2,1,0:T(8,128)(2,1)}, bf16[2,64,768]{2,1,0:T(8,128)(2,1)}, bf16[2,64,768]{2,1,0:T(8,128)(2,1)}, f32[768,768]{1,0:T(8,128)}) custom-call(bf16[2,64,768]{2,1,0:T(8,128)(2,1)} %get-tuple-element.15.mixed, bf16[2,64,768]{2,1,0:T(8,128)(2,1)} %get-tuple-element.16.dq, ...), custom_call_target="tpu_custom_call" | custom-call | tf_op jit(solution)/shard_map/pallas_call | solution.py:743

commit v8 on v6

--- a/solution.py
+++ b/solution.py
@@ -475,8 +475,6 @@
     mixed_ref[0] = mixed[:TOK]
     mixed_ref[1] = mixed[TOK:]
     stores[0].start()
-    send_beyond(1)
-    send_own(1)
 
     @pl.loop(0, 2)
     def _(s):
@@ -501,6 +499,8 @@
                 cb[0, s, i, :, lanes] = dk[i * TOK : (i + 1) * TOK]
 
     stores[1].start()
+    send_beyond(1)
+    send_own(1)
     send_outer(0)
     send_mate(0)
 

time: 65 us -> 64.8 us (level)
  no operation moved by 1% of the time
where the time goes in v8:
time: 64.8 us; the launch traced here: 64.7 us
  Pallas kernels  64 us (99%)
    pallas_call x1, Pallas kernels, on_device(): pl.pallas_call(kernel, out_shape=(blocks, blocks, blocks, blocks, jax.Sha...  61.1 us
    pallas_call x1, Pallas kernels, on_device(): pl.pallas_call(finish, out_shape=(blocks, blocks, blocks, blocks, jax.Sha...  2.9 us

profile of v8, /device:TPU:1, one launch (start us, length us, event | category | flops | bytes accessed | tf_op | source)
XLA Modules:
  0.0 64.7 jit_solution(13537735429972388864)
XLA Ops:
  0.6 61.1 %shard_map.110 = (bf16[2,64,768]{2,1,0:T(8,128)(2,1)}, bf16[2,64,768]{2,1,0:T(8,128)(2,1)}, bf16[2,64,768]{2,1,0:T(8,128)(2,1)}, bf16[2,64,768]{2,1,0:T(8,128)(2,1)}, bf16[2,2304,128]{2,1,0:T(8,128)(2,1)}) custom-call(bf16[2,64,768]{2,1,0:T(8,128)(2,1)} %bitcast.9, bf16[2,64,768]{2,1,0:T(8,128)(2,1)} %bitcast.10, bf16[2,64,768]{2,1,0:T(8,128)(2,1)} %bitcast.11, ...), custom_call_target="tpu_custom_call" | custom-call | tf_op jit(solution)/shard_map/pallas_call | solution.py:660
  61.8 2.9 %shard_map.111 = (bf16[2,64,768]{2,1,0:T(8,128)(2,1)}, bf16[2,64,768]{2,1,0:T(8,128)(2,1)}, bf16[2,64,768]{2,1,0:T(8,128)(2,1)}, bf16[2,64,768]{2,1,0:T(8,128)(2,1)}, f32[768,768]{1,0:T(8,128)}) custom-call(bf16[2,64,768]{2,1,0:T(8,128)(2,1)} %get-tuple-element.15.mixed, bf16[2,64,768]{2,1,0:T(8,128)(2,1)} %get-tuple-element.16.dq, ...), custom_call_target="tpu_custom_call" | custom-call | tf_op jit(solution)/shard_map/pallas_call | solution.py:736
